TPU v7x, 128 devices: a whole 4x4x4 slice. The times are simulated.
128 devices in a mesh: grp: 16 (over y, x), tp: 8 (over z, core).
Axes of the slice: x: 4, y: 4, z: 4, core: 2. Of those that a mesh axis runs over, the one named last changes fastest.
Arguments:
- prompt_len: int32 [256], replicated, may hold values from 1 to 1022, 131072 in all
- request_owner: int32 [16, 16], replicated, may hold values from 0 to 15, each once within a row
- page_table: int32 [16, 128], P('grp'), may hold values from 0 to 127, each once within a row
- kv_pool: bfloat16 [2048, 2, 8, 128, 128], P('grp', None, 'tp'), may hold values from -400 to 400
- step_input: bfloat16 [2, 256, 8192], P(None, None, 'grp'), may hold values from -250 to 250
- norm_gain: bfloat16 [8192], P('grp'), may hold values from 0.5 to 1.5
- w_qkv: bfloat16 [8192, 8, 1280], P('grp', 'tp'), may hold values from -1 to 1
- w_out: bfloat16 [8, 1024, 8192], P('tp', None, 'grp'), may hold values from -0.375 to 0.375
Outputs:
- attn_out: bfloat16 [2, 256, 8192], P(None, None, 'grp')
- decode_cache: bfloat16 [256, 8, 2, 8, 128, 128], P('grp', None, None, 'tp')
Inputs may be any that keep to these rules, and one draw needn't show every extreme that they name: `request_owner`: each row names every decode group once: each prefill shard hands one request to each group. `page_table`: each row holds each page slot of its prefill shard once; slot j of the shard keeps its page p at entry j * 8 + p.
All inputs are finite; a program needn't handle non-finite values.
Results may differ from a plain program's by a relative error of at most 0.005.
The roundings to bfloat16 on the way count: a program that leaves them out, or rounds other values in their place, can miss the bound.
Values may be sent and summed in bfloat16 or wider, within the bound.
No kernel may reach another device: no remote copies, remote signals or barrier semaphores. Data moves between devices by JAX's collectives and lax.ppermute only.
A program may use at most 128 MiB of HBM per device.

v0:
```python
import math

import jax
import jax.numpy as jnp
from jax import lax
from jax.sharding import PartitionSpec as P

D = 8192


epsilon = 1e-05
negative_big = -1e30


def page_stats(queries, key_rows, value_rows, valid_mask):
    score_scale = 1.0 / math.sqrt(queries.shape[-1])
    scores = (
        jnp.einsum("nskge,npkie->npskgi", queries, key_rows, preferred_element_type=jnp.float32)
        * score_scale
    )
    allowed = valid_mask[:, :, :, None, None, :]
    top_score = jnp.max(jnp.where(allowed, scores, negative_big), axis=-1)
    exponent = jnp.where(allowed, jnp.exp(scores - top_score[..., None]), 0.0)
    weight_sum = jnp.sum(exponent, axis=-1)
    weighted = jnp.einsum(
        "npskgi,npkie->npskge",
        exponent.astype(jnp.bfloat16),
        value_rows,
        preferred_element_type=jnp.float32,
    )
    return (top_score, weight_sum, weighted)


def fresh_block(queries, key_new, value_new):
    step_count = key_new.shape[1]
    key_rows = jnp.transpose(key_new, (0, 2, 1, 3))[:, None]
    value_rows = jnp.transpose(value_new, (0, 2, 1, 3))[:, None]
    step_ids = jnp.arange(step_count, dtype=jnp.int32)
    valid_mask = (step_ids[None, :] <= step_ids[:, None])[None, None]
    return page_stats(queries, key_rows, value_rows, valid_mask)


def combine(partials):
    top_score = jnp.concatenate([partial_stat[0] for partial_stat in partials], axis=1)
    weight_sum = jnp.concatenate([partial_stat[1] for partial_stat in partials], axis=1)
    weighted = jnp.concatenate([partial_stat[2] for partial_stat in partials], axis=1)
    best_score = jnp.max(top_score, axis=1, keepdims=True)
    factor = jnp.exp(top_score - best_score)
    numerator = jnp.sum(weighted * factor[..., None], axis=1)
    denominator = jnp.sum(weight_sum * factor, axis=1)
    return (numerator / denominator[..., None]).astype(jnp.bfloat16)


def insert_tokens(page_data, lengths, key_new, value_new):
    page_count = page_data.shape[1]
    page_len = page_data.shape[4]
    step_count = key_new.shape[1]
    positions = jnp.arange(page_count * page_len, dtype=jnp.int32).reshape(page_count, page_len)
    target = lengths[:, None] + jnp.arange(step_count, dtype=jnp.int32)[None, :]
    new_marks = (positions[None, None] == target[:, :, None, None]).astype(jnp.bfloat16)
    fresh_rows = jnp.stack((key_new, value_new), axis=2)
    new_tokens = jnp.einsum(
        "nspi,nscke->npckie", new_marks, fresh_rows, preferred_element_type=jnp.float32
    )
    return page_data + new_tokens.astype(jnp.bfloat16)


def per_device(prompt_len, request_owner, page_table, kv_pool, step_input, norm_gain, w_qkv, w_out):
    groups = lax.axis_size("grp")
    device_row = lax.axis_index("grp")
    step_count = step_input.shape[0]
    local_width = step_input.shape[2]
    kv_local = w_qkv.shape[1]
    head_dim = kv_pool.shape[-1]
    page_len = kv_pool.shape[-2]
    max_pages = page_table.shape[1] // groups
    group_heads = w_out.shape[1] // head_dim
    slot_ids = jnp.arange(groups, dtype=jnp.int32)
    slot_of = jnp.sum(
        slot_ids[None, :, None] * (request_owner[:, :, None] == slot_ids[None, None, :]), axis=1
    )
    send_order = lax.dynamic_index_in_dim(slot_of, device_row, 0, keepdims=False)
    values_x = step_input.astype(jnp.float32)
    squares = jnp.sum(values_x * values_x, axis=-1)
    normed = (values_x * norm_gain.astype(jnp.float32)).astype(jnp.bfloat16)
    flat_weight = w_qkv.reshape(local_width, -1)
    partial_proj = jnp.einsum(
        "srd,dc->src", normed, flat_weight, preferred_element_type=jnp.float32
    )
    projected, square_sum = lax.psum((partial_proj, squares), "grp")
    source_slots = lax.dynamic_index_in_dim(slot_of, device_row, 1, keepdims=False)
    row_ids = slot_ids * groups + source_slots
    projected = jnp.transpose(jnp.take(projected, row_ids, axis=1), (1, 0, 2))
    square_sum = jnp.transpose(jnp.take(square_sum, row_ids, axis=1))
    inv_rms = lax.rsqrt(square_sum / D + epsilon)
    projected = (projected * inv_rms[:, :, None]).reshape(
        groups, step_count, kv_local, (group_heads + 2) * head_dim
    )
    queries = (
        projected[..., : group_heads * head_dim]
        .reshape(groups, step_count, kv_local, group_heads, head_dim)
        .astype(jnp.bfloat16)
    )
    key_new = projected[..., group_heads * head_dim : (group_heads + 1) * head_dim].astype(
        jnp.bfloat16
    )
    value_new = projected[..., (group_heads + 1) * head_dim :].astype(jnp.bfloat16)
    lengths = jnp.take(prompt_len, row_ids)
    page_ids = page_table.reshape(groups, max_pages)
    pool_ids = jnp.take(page_ids, send_order, axis=0)
    send_lengths = jnp.take(prompt_len, device_row * groups + send_order)
    page_data = jnp.take(kv_pool, pool_ids.reshape(-1), axis=0).reshape(
        (groups, max_pages) + kv_pool.shape[1:]
    )
    positions = jnp.arange(max_pages * page_len, dtype=jnp.int32).reshape(max_pages, page_len)
    send_valid = positions[None] < send_lengths[:, None, None]
    page_data = jnp.where(
        send_valid[:, :, None, None, :, None], page_data, jnp.zeros((), page_data.dtype)
    )
    counts = jnp.clip(send_lengths[:, None] - positions[None, :, 0], 0, page_len).astype(
        jnp.bfloat16
    )
    page_piece = lax.all_to_all(page_data, "grp", split_axis=0, concat_axis=0, tiled=True)
    count_piece = lax.all_to_all(counts, "grp", split_axis=0, concat_axis=0, tiled=True)
    inside = (
        jnp.arange(page_len, dtype=jnp.float32)[None, None, :]
        < count_piece.astype(jnp.float32)[:, :, None]
    )
    page_result = page_stats(
        queries, page_piece[:, :, 0], page_piece[:, :, 1], inside[:, :, None, :]
    )
    arrived_pages, top_score, weight_sum, weighted = (page_piece,) + page_result
    head_rows = combine(
        [(top_score, weight_sum, weighted), fresh_block(queries, key_new, value_new)]
    )
    decode_cache = insert_tokens(arrived_pages, lengths, key_new, value_new)
    head_rows = head_rows.reshape(groups, step_count, kv_local * group_heads * head_dim)
    out_weight = w_out.reshape(kv_local * group_heads * head_dim, local_width)
    partial_out = jnp.einsum(
        "nsf,fd->nsd",
        lax.all_gather(head_rows, "grp", axis=0, tiled=True),
        out_weight,
        preferred_element_type=jnp.float32,
    )
    summed = lax.psum(partial_out, "tp")
    back_order = (request_owner * groups + slot_ids[:, None]).reshape(-1)
    summed = jnp.take(summed, back_order, axis=0)
    return (jnp.transpose(summed, (1, 0, 2)).astype(jnp.bfloat16), decode_cache)


def solution(mesh):
    placed = (
        P(),
        P(),
        P("grp", None),
        P("grp", None, "tp", None, None),
        P(None, None, "grp"),
        P("grp"),
        P("grp", "tp", None),
        P("tp", None, "grp"),
    )
    return jax.shard_map(
        per_device,
        mesh=mesh,
        in_specs=placed,
        out_specs=(P(None, None, "grp"), P("grp", None, None, "tp", None, None)),
        check_vma=False,
    )
```

profile of v0, /device:TPU:0, one launch (start us, length us, event | category | flops | bytes accessed | tf_op | source)
XLA Modules:
  0.0 378.3 jit_solution(5244458971284694277)
XLA Ops:
  7.2 0.9 select_reduce_fusion.2
  8.3 1.3 gather_fusion.5
  9.9 0.7 copy.126
  10.6 7.1 %all-to-all-start.1 = ((bf16[16,1,8]{2,1,0:T(2,128)(2,1)}), bf16[16,1,8]{2,1,0:T(2,128)(2,1)S(1)}, u32[]{:S(2)}, u32[]{:S(2)}) async-start(bf16[16,1,8]{2,1,0:T(2,128)(2,1)} %copy.126), calls=%async_computation.1 | async-start | bytes 16384 | tf_op jit(solution)/shard_map/all_to_all | solution.py:124
  17.8 0.5 broadcast.427
  18.4 1.3 reduce.27
  20.0 0.6 gather_fusion
  20.7 10.1 %gather_fusion.1 = bf16[128,2,128,128]{3,2,1,0:T(8,128)(2,1)} fusion(bf16[128,2,128,128]{3,2,1,0:T(8,128)(2,1)} %bitcast.133, s32[1024]{0:T(1024)S(1)} %pad_clamp_fusion.3), kind=kCustom, calls=%fused_computation.3 | custom fusion | bytes 16777728 | tf_op jit(solution)/shard_map/jit(_take)/gather | solution.py:112
  30.9 8.0 %select_select_fusion = bf16[16,8,2,1,128,128]{5,4,2,1,0,3:T(8,128)(2,1)} fusion(bf16[16,8,2,1,128,128]{5,4,2,1,0,3:T(8,128)(2,1)} %bitcast.132, pred[16,8]{1,0:T(8,128)(4,1)S(1)} %get-tuple-element.23, pred[16,8,128]{2,1,0:T(8,128)(4,1)S(1)} %broadcast_compare_fusion), kind=kLoop, calls=%fused_computation.8 | loop fusion | flops 8388608 | bytes 16793728 | tf_op jit(solution)/shard_map/jit(_where)/select_n | solution.py:117
  38.9 10.3 %copy.124 = bf16[16,8,2,1,128,128]{5,4,1,3,2,0:T(8,128)(2,1)} copy(bf16[16,8,2,1,128,128]{5,4,2,1,0,3:T(8,128)(2,1)} %select_select_fusion) | data formatting | bytes 16777216 | tf_op jit(solution)/shard_map/jit(_where)/select_n | solution.py:117
  49.2 7.4 %all-to-all-start = ((bf16[16,8,2,1,128,128]{5,4,1,3,2,0:T(8,128)(2,1)}), bf16[16,8,2,1,128,128]{5,4,1,3,2,0:T(8,128)(2,1)}, u32[]{:S(2)}, u32[]{:S(2)}) async-start(bf16[16,8,2,1,128,128]{5,4,1,3,2,0:T(8,128)(2,1)} %copy.124), calls=%async_computation | async-start | bytes 16777216 | tf_op jit(solution)/shard_map/all_to_all | solution.py:123
  56.8 2.3 fusion.5
  59.7 193.7 %psum.22 = f32[2,256]{0,1:T(8,128)S(1)} all-reduce(f32[2,256]{0,1:T(8,128)S(1)} %copy.131), channel_id=1, replica_groups=mesh['grp'=16,'tp'=8] {'grp'}, use_global_device_ids=true, to_apply=%region_3.0 | all-reduce | flops 512 | bytes 4096 | tf_op jit(solution)/shard_map/psum | solution.py:90
  253.4 0.6 gather_fusion.3
  254.5 5.3 %copy.130 = f32[2,256,1280]{2,0,1:T(2,128)} copy(f32[2,256,1280]{2,1,0:T(8,128)} %all-reduce.3.cloned.1.call-done) | data formatting | bytes 5242880 | tf_op jit(solution)/shard_map/psum | solution.py:90
  259.7 2.5 gather_fusion.2
  262.6 0.4 select_reduce_fusion.3
  263.4 3.6 select_reduce_fusion
  267.0 0.8 bitcast_reduce_fusion
  268.0 3.5 fusion.2
  272.2 0.6 copy.146
  272.9 0.7 gather_fusion.6
  273.7 12.3 %copy.136 = bf16[16,8,2,1,128,128]{4,5,1,2,0,3:T(8,128)(2,1)} copy(bf16[16,8,2,1,128,128]{5,4,1,3,2,0:T(8,128)(2,1)} %all-to-all-done) | data formatting | bytes 16777216 | tf_op jit(solution)/shard_map/all_to_all | solution.py:123
  285.9 9.0 %bitcast_add_fusion = bf16[16,8,2,1,128,128]{4,5,1,2,0,3:T(8,128)(2,1)} fusion(bf16[16,8,2,1,128,128]{4,5,1,2,0,3:T(8,128)(2,1)} %copy.136, s32[16,2]{1,0:T(8,128)S(1)} %iota_add_fusion, s32[8,128]{1,0:T(8,128)S(1)} %multiply_add_fusion, bf16[16,2,1,1,128]{4,1,0,3,2:T(2,128)(2,1)S(1)} %get-tuple-element.26, bf16[16,2,1,1,128]{4,1,0,3,2:T(2,128)(2,1)S(1)} %get-tuple-element.25), kind=kOutput, calls=%fused_computation.7 | convolution fusion | flops 25206784 | bytes 16797824 | tf_op jit(solution)/shard_map/nspi,nscke->npckie/dot_general | solution.py:62
  295.0 12.4 %copy.138 = bf16[16,8,2,1,128,128]{5,4,3,2,1,0:T(8,128)(2,1)} copy(bf16[16,8,2,1,128,128]{4,5,1,2,0,3:T(8,128)(2,1)} %bitcast_add_fusion) | data formatting | bytes 16777216
  307.3 6.3 %all-gather.2.cloned.1.call-done = bf16[256,2,1024]{2,0,1:T(8,128)(2,1)} async-done(((bf16[16,2,1024]{2,0,1:T(8,128)(2,1)}), bf16[256,2,1024]{2,0,1:T(8,128)(2,1)}) %all-gather.2.cloned.1.call-update) | async-done | bytes 1048592 | tf_op jit(solution)/shard_map/all_gather | solution.py:141
  313.6 2.2 fusion.11
  315.9 51.4 %all-reduce.4 = bf16[256,2,512]{2,0,1:T(8,128)(2,1)S(1)} all-reduce(f32[256,2,512]{2,0,1:T(8,128)S(1)} %fusion.11), channel_id=1, replica_groups=mesh['grp'=16,'tp'=8] {'tp'}, use_global_device_ids=true, to_apply=%region_11.13 | all-reduce | flops 262144 | bytes 1572864 | tf_op jit(solution)/shard_map/psum | solution.py:145
  367.3 0.5 copy.134
  367.8 1.7 gather_fusion.4
  369.6 1.1 fusion.19
  370.6 0.8 copy.137
  (70 shorter events, 3.9 us)
Async XLA Ops:
  7.2 49.6 %copy-start = (bf16[512,1,1280]{2,0,1:T(8,128)(2,1)S(1)}, bf16[512,1,1280]{2,0,1:T(8,128)(2,1)}, u32[]{:S(2)}) copy-start(bf16[512,1,1280]{2,0,1:T(8,128)(2,1)} %param.16) | copy-start | bytes 3932164
  10.6 38.7 %all-to-all-start.1 = ((bf16[16,1,8]{2,1,0:T(2,128)(2,1)}), bf16[16,1,8]{2,1,0:T(2,128)(2,1)S(1)}, u32[]{:S(2)}, u32[]{:S(2)}) async-start(bf16[16,1,8]{2,1,0:T(2,128)(2,1)} %copy.126), calls=%async_computation.1 | async-start | bytes 16384 | tf_op jit(solution)/shard_map/all_to_all | solution.py:124
  49.2 7.5 %copy-start.5 = (bf16[512]{0:T(512)(128)(2,1)S(1)}, bf16[512]{0:T(512)(128)(2,1)}, u32[]{:S(2)}) copy-start(bf16[512]{0:T(512)(128)(2,1)} %param.15) | copy-start | bytes 3076
  49.2 7.5 %copy-start.3 = (bf16[2,256,512]{2,1,0:T(8,128)(2,1)S(1)}, bf16[2,256,512]{2,1,0:T(8,128)(2,1)}, u32[]{:S(2)}) copy-start(bf16[2,256,512]{2,1,0:T(8,128)(2,1)} %param.14) | copy-start | bytes 1572868
  49.2 9.9 %copy-start.4 = (s32[16,16]{1,0:T(8,128)S(1)}, s32[16,16]{1,0:T(8,128)}, u32[]{:S(2)}) copy-start(s32[16,16]{1,0:T(8,128)} %param.11) | copy-start | bytes 3076
  49.2 214.2 %all-to-all-start = ((bf16[16,8,2,1,128,128]{5,4,1,3,2,0:T(8,128)(2,1)}), bf16[16,8,2,1,128,128]{5,4,1,3,2,0:T(8,128)(2,1)}, u32[]{:S(2)}, u32[]{:S(2)}) async-start(bf16[16,8,2,1,128,128]{5,4,1,3,2,0:T(8,128)(2,1)} %copy.124), calls=%async_computation | async-start | bytes 16777216 | tf_op jit(solution)/shard_map/all_to_all | solution.py:123
  56.7 197.8 %all-reduce.3.cloned.1.call-start = ((), (), s32[]{:S(2)}) async-start(), calls=%async_computation.2 | async-start | bytes 5242880 | tf_op jit(solution)/shard_map/psum | solution.py:90
  59.1 254.5 %all-gather.2.cloned.1.call-start = ((), (), s32[]{:S(2)}) async-start(), calls=%async_computation.3 | async-start | bytes 1114112 | tf_op jit(solution)/shard_map/all_gather | solution.py:141
  263.4 9.5 %copy-start.2 = (s32[256]{0:T(256)S(1)}, s32[256]{0:T(256)}, u32[]{:S(2)}) copy-start(s32[256]{0:T(256)} %param.10) | copy-start | bytes 3076
  295.0 76.5 %copy-start.1 = (bf16[512,1,1280]{2,0,1:T(8,128)(2,1)S(1)}, bf16[512,1,1280]{2,0,1:T(8,128)(2,1)}, u32[]{:S(2)}) copy-start(bf16[512,1,1280]{2,0,1:T(8,128)(2,1)} %param.16) | copy-start | bytes 3932164
Sparse Core Ops, SparseCore 0:
  61.4 176.4 all-reduce.2
  273.0 40.5 all-gather.1
where the time goes:
time: 380 us; the launch traced here: 378 us
  blocking collectives  245 us (64%)
  local copies, waits for them, and re-layouts  62 us (16%)
  matrix products  21.3 us (6%)
  other arithmetic  14.6 us (4%)
  starting transfers between devices  14.6 us (4%)
  between operations  14.4 us (4%)
  waiting for transfers between devices  6.34 us (2%)
    psum x1, blocking collectives, per_device(): projected, square_sum = lax.psum((partial_proj, squares), 'grp')  194 us
    psum x1, blocking collectives, per_device(): summed = lax.psum(partial_out, 'tp')  51.4 us
    unnamed x15, local copies, waits for them, and re-layouts  13.8 us
    all_to_all x1, local copies, waits for them, and re-layouts, per_device(): lax.all_to_all(page_data, 'grp', split_axis=0, concat_axis=0, tiled=True)  12.3 us
    select_n x1, local copies, waits for them, and re-layouts, per_device(): jnp.where(send_valid[:, :, None, None, :, None], page_data, jnp.zeros((),...  10.3 us
    gather x1, local copies, waits for them, and re-layouts, per_device(): jnp.take(kv_pool, pool_ids.reshape(-1), axis=0)  10.1 us
    dot_general x1, matrix products, insert_tokens(): jnp.einsum('nspi,nscke->npckie', new_marks, fresh_rows, preferred_element...  9.03 us
    select_n x1, other arithmetic, per_device(): jnp.where(send_valid[:, :, None, None, :, None], page_data, jnp.zeros((),...  8.04 us
  transfers between devices with their start and end apart: 4, of which 1 were waited for; matrix products, arithmetic and copies ran while one was open for 21% of the time, Pallas kernels for 0%

commit v1 on v0

v1 whole, which is shorter than its diff:
```python
import functools
import math

import jax
import jax.numpy as jnp
from jax import lax
from jax.experimental import pallas as pl
from jax.experimental.pallas import tpu as pltpu
from jax.sharding import PartitionSpec as P

D = 8192
PAGE = 128
HD = 128
MAXP = 8
STEPS = 2
TILE = 16
CORES = 2
SIDE = 4
SLOTS = 16
ROWS = STEPS * SLOTS
CUTS = (0, 4, 8)
OWNER, LENGTH, TABLE = 0, 256, 512

epsilon = 1e-05
negative_big = -1e30

HBM = pl.BlockSpec(memory_space=pltpu.HBM)
ANY = pl.BlockSpec(memory_space=pl.ANY)
SMEM = pl.BlockSpec(memory_space=pltpu.SMEM)
VMEM = pl.BlockSpec(memory_space=pltpu.VMEM)


def params(mib):
    return pltpu.CompilerParams(vmem_limit_bytes=mib * 2**20)


def cost(flops, moved):
    return pl.CostEstimate(flops=flops, bytes_accessed=moved, transcendentals=0)


def move_part(array, dz, dc):
    pairs = [(z * CORES + c, ((z + dz) % SIDE) * CORES + (c + dc) % CORES) for z in range(SIDE) for c in range(CORES)]
    return lax.ppermute(array, "tp", pairs)


def project_kernel(x_ref, gain_ref, w_ref, out_ref):
    shards = out_ref.shape[0]
    blocks = w_ref.shape[1] // HD
    gain = gain_ref[...].astype(jnp.float32)
    for st in range(STEPS):
        x = x_ref[st].astype(jnp.float32)
        squares = jnp.broadcast_to(jnp.sum(x * x, axis=-1, keepdims=True), (x.shape[0], HD))
        acc = jnp.dot((x * gain).astype(jnp.bfloat16), w_ref[...], preferred_element_type=jnp.float32)
        for c in range(blocks):
            out_ref[:, pl.ds(c * ROWS + st * SLOTS, SLOTS), :] = acc[:, c * HD:(c + 1) * HD].reshape(shards, SLOTS, HD)
        half = 8 // STEPS
        per = HD // SLOTS
        for t in range(x.shape[0] // HD):
            lanes = jnp.transpose(squares[t * HD:(t + 1) * HD])[:half]
            out_ref[t * per:(t + 1) * per, pl.ds(blocks * ROWS + st * half, half), :] = jnp.broadcast_to(lanes[None], (per, half, HD))


def project(x, gain, w, shards):
    blocks = w.shape[1] // HD
    return pl.pallas_call(
        project_kernel,
        out_shape=jax.ShapeDtypeStruct((shards, blocks * ROWS + 8, HD), jnp.float32),
        in_specs=[VMEM, VMEM, VMEM],
        out_specs=VMEM,
        compiler_params=params(40),
        cost_estimate=cost(2 * 512 * 512 * 1280, 6 * 2**20),
        name="project",
    )(x, gain, w)


def slot_for(ints_ref, shard, group):
    def look(j, found):
        return jnp.where(ints_ref[OWNER + shard * SLOTS + j] == group, j, found)
    return lax.fori_loop(0, SLOTS, look, 0)


def gather_kernel(low, ints_ref, pool_ref, out_ref, sems):
    me = lax.axis_index("grp")
    count = out_ref.shape[1]

    def request(j):
        return ints_ref[OWNER + me * SLOTS + j], ints_ref[LENGTH + me * SLOTS + j] - low * PAGE

    def load(j, g, p):
        return pltpu.make_async_copy(pool_ref.at[ints_ref[TABLE + j * MAXP + low + p], :, 0], out_ref.at[g, p], sems.at[j, p])

    def start(j, carry):
        g, left = request(j)
        for p in range(count):
            @pl.when(p * PAGE < left)
            def _():
                load(j, g, p).start()

            @pl.when(p * PAGE >= left)
            def _():
                out_ref[g, p] = jnp.zeros(out_ref.shape[2:], out_ref.dtype)
        return carry

    def finish(j, carry):
        g, left = request(j)
        for p in range(count):
            @pl.when(p * PAGE < left)
            def _():
                load(j, g, p).wait()

        @pl.when((left > 0) & (left < count * PAGE))
        def _():
            edge = (left - 1) // PAGE
            rows = lax.broadcasted_iota(jnp.int32, (2, PAGE, HD), 1)
            page = jnp.where(rows < left - edge * PAGE, out_ref[g, edge].astype(jnp.float32), 0.0)
            out_ref[g, edge] = page.astype(out_ref.dtype)
        return carry

    lax.fori_loop(0, SLOTS, start, 0)
    lax.fori_loop(0, SLOTS, finish, 0)


def gather_pages(low, high, ints, pool):
    shape = jax.ShapeDtypeStruct((SLOTS, high - low, 2, PAGE, HD), jnp.bfloat16)
    return pl.pallas_call(
        functools.partial(gather_kernel, low),
        out_shape=shape,
        in_specs=[SMEM, ANY],
        out_specs=VMEM,
        scratch_shapes=[pltpu.SemaphoreType.DMA((SLOTS, high - low))],
        compiler_params=params(44),
        cost_estimate=cost(0, (high - low) * 2**21),
        name="gather_pages",
    )(ints, pool)


def attend_kernel(ints_ref, *refs):
    sums_ref, pool_ref, out_ref, proj, done = refs
    me = lax.axis_index("grp")
    step = pl.program_id(0)
    block = SLOTS // pl.num_programs(0)
    scale = 1.0 / math.sqrt(HD)
    heads = out_ref.shape[2] // HD - 2
    blocks = heads + 2
    qr = STEPS * heads

    @pl.when(step == 0)
    def _():
        total = sums_ref[0]
        for i in range(1, sums_ref.shape[0]):
            total = total + sums_ref[i]
        half = 8 // STEPS
        shape = (SLOTS, HD)
        mine = lax.broadcasted_iota(jnp.int32, shape, 1) == (me % (HD // SLOTS)) * SLOTS + lax.broadcasted_iota(jnp.int32, shape, 0)
        squares = []
        for st in range(STEPS):
            row = total[blocks * ROWS + st * half:blocks * ROWS + st * half + 1]
            squares.append(jnp.sum(jnp.where(mine, jnp.broadcast_to(row, shape), 0.0), axis=-1, keepdims=True))
        inv_rms = lax.rsqrt(jnp.concatenate(squares, axis=0) / D + epsilon)
        for c in range(blocks):
            proj[c * ROWS:(c + 1) * ROWS, :] = (total[c * ROWS:(c + 1) * ROWS] * inv_rms).astype(jnp.bfloat16).astype(jnp.float32)

    lanes = lax.broadcasted_iota(jnp.int32, (qr, PAGE), 1)
    later = lax.broadcasted_iota(jnp.int32, (qr, 1), 0) % STEPS > 0
    contract = (((1,), (1,)), ((), ()))
    slots, pages, queries, scores = [], [], [], []
    for r in range(block):
        j = step * block + r
        q = proj[pl.ds(j, qr, stride=SLOTS), :]
        ids = [ints_ref[TABLE + j * MAXP + p] for p in range(MAXP)]
        slots.append(j)
        pages.append(ids)
        queries.append(q)
        scores.append([lax.dot_general(q.astype(jnp.bfloat16), pool_ref[i, 0, 0], contract, preferred_element_type=jnp.float32) * scale for i in ids])
    allowed, tops, exps, totals = [], [], [], []
    for r in range(block):
        length = ints_ref[LENGTH + me * SLOTS + slots[r]]
        allowed.append([lanes < length - p * PAGE for p in range(MAXP)])
        tops.append([jnp.max(jnp.where(ok, sc, negative_big), axis=-1, keepdims=True) for ok, sc in zip(allowed[r], scores[r])])
    for r in range(block):
        exps.append([jnp.where(ok, jnp.exp(sc - top), 0.0) for ok, sc, top in zip(allowed[r], scores[r], tops[r])])
        totals.append([jnp.sum(e, axis=-1, keepdims=True) for e in exps[r]])
    parts = []
    for r in range(block):
        parts.append([jnp.dot(e.astype(jnp.bfloat16), pool_ref[i, 1, 0], preferred_element_type=jnp.float32) for e, i in zip(exps[r], pages[r])])
    for r in range(block):
        j, q = slots[r], queries[r]
        key = [proj[pl.ds(heads * ROWS + s * SLOTS + j, 1), :] for s in range(STEPS)]
        value = [proj[pl.ds((heads + 1) * ROWS + s * SLOTS + j, 1), :] for s in range(STEPS)]
        fresh = [jnp.sum(q * k, axis=-1, keepdims=True) * scale for k in key]
        top = jnp.where(later, jnp.maximum(fresh[0], fresh[1]), fresh[0])
        e = [jnp.exp(fresh[0] - top), jnp.where(later, jnp.exp(fresh[1] - top), 0.0)]
        part = sum(w.astype(jnp.bfloat16).astype(jnp.float32) * v for w, v in zip(e, value))
        best = top
        for t in tops[r]:
            best = jnp.maximum(best, t)
        above, below = 0.0, 0.0
        for t, total, p in zip(tops[r] + [top], totals[r] + [e[0] + e[1]], parts[r] + [part]):
            factor = jnp.exp(t - best)
            above = above + p * factor
            below = below + total * factor
        done[pl.ds(j, qr, stride=SLOTS), :] = above / below

    @pl.when(step == pl.num_programs(0) - 1)
    def _():
        for c in range(blocks):
            source = done if c < heads else proj
            part = source[c * ROWS:(c + 1) * ROWS, :].astype(out_ref.dtype)
            for g in range(out_ref.shape[0]):
                out_ref[g, :, c * HD:(c + 1) * HD] = part


def attend(ints, sums, pool):
    blocks = sums.shape[1] // ROWS
    whole = lambda a: pl.BlockSpec(a.shape, lambda i, *_: (0,) * len(a.shape))
    out = jax.ShapeDtypeStruct((sums.shape[0], ROWS, blocks * HD), jnp.bfloat16)
    return pl.pallas_call(
        attend_kernel,
        out_shape=out,
        grid_spec=pltpu.PrefetchScalarGridSpec(
            num_scalar_prefetch=1,
            grid=(4,),
            in_specs=[VMEM, VMEM],
            out_specs=whole(out),
            scratch_shapes=[pltpu.VMEM((blocks * ROWS, HD), jnp.float32), pltpu.VMEM(((blocks - 2) * ROWS, HD), jnp.float32)],
        ),
        compiler_params=params(24),
        cost_estimate=cost(4 * SLOTS * MAXP * PAGE * HD * 16, 10 * 2**20),
        name="attend",
    )(ints, sums, pool)


def output_kernel(rows_ref, w_ref, *refs):
    outs, box = refs[:-1], refs[-1]
    part = lax.axis_index("tp")
    z, core = part // CORES, part % CORES
    each = rows_ref.shape[0] // box.shape[0]
    for b in range(box.shape[0]):
        lhs = rows_ref[b * each:(b + 1) * each].reshape(each * ROWS, -1)[:, :w_ref.shape[0]]
        box[b] = jnp.dot(lhs, w_ref[...], preferred_element_type=jnp.float32)
    for i, out in enumerate(outs):
        dz, dc = divmod(i, CORES)
        out[...] = box[((z + dz) % SIDE) * CORES + (core + dc) % CORES]


def output_rows(rows, w):
    parts = SIDE * CORES
    shape = jax.ShapeDtypeStruct((rows.shape[0] * ROWS // parts, w.shape[1]), jnp.float32)
    return pl.pallas_call(
        output_kernel,
        out_shape=[shape] * parts,
        in_specs=[VMEM, VMEM],
        out_specs=[VMEM] * parts,
        scratch_shapes=[pltpu.VMEM((parts,) + shape.shape, jnp.float32)],
        compiler_params=params(24),
        cost_estimate=cost(2 * 512 * 512 * 1024, 4 * 2**20),
        name="output_rows",
    )(rows, w)


def total_kernel(*refs):
    ins, out = refs[:-1], refs[-1]
    while len(ins) > 1:
        ins = [ins[i][...] + ins[i + 1][...] for i in range(0, len(ins), 2)]
    out[...] = ins[0].astype(out.dtype)


def total_rows(arrays):
    return pl.pallas_call(
        total_kernel,
        out_shape=jax.ShapeDtypeStruct(arrays[0].shape, jnp.bfloat16),
        in_specs=[VMEM] * len(arrays),
        out_specs=VMEM,
        cost_estimate=cost(0, 2**20),
        name="total_rows",
    )(*arrays)


def order_kernel(*refs):
    ins, out = refs[:-1], refs[-1]
    part = lax.axis_index("tp")
    z, core = part // CORES, part % CORES
    for i, source in enumerate(ins):
        dz, dc = divmod(i, CORES)
        block = ((z - dz + SIDE) % SIDE) * CORES + (core + dc) % CORES
        each = source.shape[0] // ROWS
        for h in range(each):
            row = pl.multiple_of((block * each + h) * SLOTS, SLOTS)
            for st in range(STEPS):
                out[st, pl.ds(row, SLOTS), :] = source[h * ROWS + st * SLOTS:h * ROWS + (st + 1) * SLOTS, :]


def order_rows(arrays):
    parts = len(arrays)
    rows, width = arrays[0].shape
    return pl.pallas_call(
        order_kernel,
        out_shape=jax.ShapeDtypeStruct((STEPS, parts * rows // STEPS, width), jnp.bfloat16),
        in_specs=[VMEM] * parts,
        out_specs=VMEM,
        cost_estimate=cost(0, 2**20),
        name="order_rows",
    )(*arrays)


def insert_kernel(low, ints_ref, rows_ref, pages_ref, *refs):
    cache_ref, box, sems = refs[-3:]
    count = pages_ref.shape[1]
    me = lax.axis_index("grp")
    first = rows_ref.shape[-1] - 2 * HD
    tile_rows = lax.broadcasted_iota(jnp.int32, (TILE, HD), 0)
    slots = lax.broadcasted_iota(jnp.int32, (SLOTS, HD), 0)
    loads = [pltpu.make_async_copy(pages_ref.at[r], box.at[r], sems.at[0, r]) for r in range(SLOTS)]
    stores = [pltpu.make_async_copy(box.at[r], cache_ref.at[r, pl.ds(low, count), :, 0], sems.at[1, r]) for r in range(SLOTS)]
    for load in loads:
        load.start()
    for r in range(SLOTS):
        slot = slot_for(ints_ref, r, me)
        at = ints_ref[LENGTH + r * SLOTS + slot]
        base = (at // TILE) * TILE

        def fill(base):
            page = base // PAGE - low

            @pl.when((page >= 0) & (page < count))
            def _():
                row = pl.multiple_of(base - (base // PAGE) * PAGE, TILE)
                for kv in range(2):
                    tile = box[r, page, kv, pl.ds(row, TILE), :].astype(jnp.float32)
                    for s in range(STEPS):
                        column = first + kv * HD
                        block = rows_ref[r, s * SLOTS:(s + 1) * SLOTS, column:column + HD].astype(jnp.float32)
                        token = jnp.sum(jnp.where(slots == slot, block, 0.0), axis=0, keepdims=True)
                        tile = jnp.where(tile_rows == at + s - base, jnp.broadcast_to(token, (TILE, HD)), tile)
                    box[r, page, kv, pl.ds(row, TILE), :] = tile.astype(box.dtype)

        loads[r].wait()
        fill(base)

        @pl.when(at - base == TILE - 1)
        def _():
            fill(base + TILE)

        stores[r].start()
    for store in stores:
        store.wait()


def insert(low, ints, rows, pages, cache):
    before = [] if cache is None else [cache]
    return pl.pallas_call(
        functools.partial(insert_kernel, low),
        out_shape=jax.ShapeDtypeStruct((SLOTS, MAXP, 2, 1, PAGE, HD), pages.dtype),
        in_specs=[SMEM, VMEM, ANY] + [ANY] * len(before),
        out_specs=ANY,
        scratch_shapes=[pltpu.VMEM(pages.shape, pages.dtype), pltpu.SemaphoreType.DMA((2, SLOTS))],
        input_output_aliases={3: 0} if before else {},
        compiler_params=params(44),
        cost_estimate=cost(0, 2 * pages.size * 2),
        name="insert_tokens",
    )(ints, rows, pages, *before)


def exchange(array):
    return lax.all_to_all(array, "grp", split_axis=0, concat_axis=0, tiled=True)


def per_device(prompt_len, request_owner, page_table, kv_pool, step_input, norm_gain, w_qkv, w_out):
    width = step_input.shape[2]
    heads = w_out.shape[1] // HD
    blocks = w_qkv.shape[2] // HD
    ints = jnp.concatenate([request_owner.reshape(-1), prompt_len, page_table.reshape(-1)])

    partial = project(step_input, norm_gain.reshape(1, width), w_qkv.reshape(width, blocks * HD), request_owner.shape[0])
    pages = [gather_pages(low, high, ints, kv_pool) for low, high in zip(CUTS, CUTS[1:])]
    mine = attend(ints, exchange(partial), kv_pool)
    rows = exchange(mine)
    received = [exchange(lax.optimization_barrier((piece, rows))[0]) for piece in pages]

    parts = output_rows(rows, w_out.reshape(heads * HD, width))
    distances = [divmod(i, CORES) for i in range(SIDE * CORES)]
    own = total_rows([parts[0]] + [move_part(parts[i], *distances[i]) for i in range(1, len(parts))])
    attn_out = order_rows([own] + [move_part(own, *d) for d in distances[1:]])

    cache = None
    for low, piece in zip(CUTS, received):
        cache = insert(low, ints, rows, piece, cache)
    return (attn_out, cache)


def solution(mesh):
    placed = (
        P(),
        P(),
        P("grp", None),
        P("grp", None, "tp", None, None),
        P(None, None, "grp"),
        P("grp"),
        P("grp", "tp", None),
        P("tp", None, "grp"),
    )
    return jax.shard_map(
        per_device,
        mesh=mesh,
        in_specs=placed,
        out_specs=(P(None, None, "grp"), P("grp", None, None, "tp", None, None)),
        check_vma=False,
    )
```

time: 380 us -> 215 us (0.57)
  blocking collectives: 245 us -> 0 us
  waiting for transfers between devices: 6.34 us -> 132 us
  local copies, waits for them, and re-layouts: 62 us -> 15.7 us
  Pallas kernels: 0 us -> 28.4 us
  starting transfers between devices: 14.6 us -> 37 us
  matrix products: 21.3 us -> 0 us
  other arithmetic: 14.6 us -> 0.01 us
  between operations: 14.4 us -> 0.86 us
    psum x2 -> x0, blocking collectives: 245 us -> none  [the longest x1 194 us: per_device(): projected, square_sum = lax.psum((partial_proj, squares), 'grp')]
    all_to_all x2 -> x4, waiting for transfers between devices: 0.01 us -> 117 us  [exchange(): return lax.all_to_all(array, 'grp', split_axis=0, concat_axis=0, tiled=True)]
    pallas_call x0 -> x9, Pallas kernels: none -> 28.4 us  [the longest x2 10.9 us: insert(): pl.pallas_call(functools.partial(insert_kernel, low), out_shape=jax.Shape...]
    dot_general x7 -> x0, matrix products: 21.3 us -> none  [the longest x1 9.03 us: insert_tokens(): jnp.einsum('nspi,nscke->npckie', new_marks, fresh_rows, preferred_element...]
    gather x7 -> x0, local copies, waits for them, and re-layouts: 17.5 us -> none  [the longest x1 10.1 us: per_device(): jnp.take(kv_pool, pool_ids.reshape(-1), axis=0)]
    ppermute x0 -> x14, starting transfers between devices: none -> 17.1 us  [move_part(): return lax.ppermute(array, 'tp', pairs)]
    ppermute x0 -> x14, waiting for transfers between devices: none -> 14.9 us  [move_part(): return lax.ppermute(array, 'tp', pairs)]
    all_to_all x2 -> x0, local copies, waits for them, and re-layouts: 12.3 us -> none  [the longest x1 12.3 us: per_device(): lax.all_to_all(page_data, 'grp', split_axis=0, concat_axis=0, tiled=True)]
  transfers between devices with their start and end apart: 4 -> 18, of which waited for: 1 -> 13; matrix products, arithmetic and copies ran while one was open for 21% -> 0% of each run, Pallas kernels for 0% -> 8%
where the time goes in v1:
time: 215 us; the launch traced here: 214 us
  waiting for transfers between devices  132 us (61%)
  starting transfers between devices  37 us (17%)
  Pallas kernels  28.4 us (13%)
  local copies, waits for them, and re-layouts  15.7 us (7%)
    all_to_all x4, waiting for transfers between devices, exchange(): return lax.all_to_all(array, 'grp', split_axis=0, concat_axis=0, tiled=True)  117 us
    all_to_all x4, starting transfers between devices, exchange(): return lax.all_to_all(array, 'grp', split_axis=0, concat_axis=0, tiled=True)  19.9 us
    ppermute x14, starting transfers between devices, move_part(): return lax.ppermute(array, 'tp', pairs)  17.1 us
    unnamed x52, local copies, waits for them, and re-layouts  14.9 us
    ppermute x14, waiting for transfers between devices, move_part(): return lax.ppermute(array, 'tp', pairs)  14.9 us
    pallas_call x2, Pallas kernels, insert(): pl.pallas_call(functools.partial(insert_kernel, low), out_shape=jax.Shape...  10.9 us
    pallas_call x2, Pallas kernels, gather_pages(): pl.pallas_call(functools.partial(gather_kernel, low), out_shape=shape, in...  6.27 us
    pallas_call x1, Pallas kernels, attend(): pl.pallas_call(attend_kernel, out_shape=out, grid_spec=pltpu.PrefetchScal...  4.92 us
  transfers between devices with their start and end apart: 18, of which 13 were waited for; matrix products, arithmetic and copies ran while one was open for 0% of the time, Pallas kernels for 8%

profile of v1, /device:TPU:0, one launch (start us, length us, event | category | flops | bytes accessed | tf_op | source)
XLA Modules:
  0.0 214.4 jit_solution(7565274809194980029)
XLA Ops:
  4.5 1.5 copy-done.3
  6.1 7.1 %all-to-all-start = ((f32[16,328,128]{2,1,0:T(8,128)}), f32[16,328,128]{2,1,0:T(8,128)S(1)}, u32[]{:S(2)}, u32[]{:S(2)}) async-start(f32[16,328,128]{2,1,0:T(8,128)} %copy-done.3), calls=%async_computation | async-start | bytes 5373952 | tf_op jit(solution)/shard_map/all_to_all | solution.py:365
  13.3 40.6 %all-to-all-done.refs_0_ = f32[16,328,128]{2,1,0:T(8,128)S(1)} async-done(((f32[16,328,128]{2,1,0:T(8,128)}), f32[16,328,128]{2,1,0:T(8,128)S(1)}, u32[]{:S(2)}, u32[]{:S(2)}) %all-to-all-start) | async-done | bytes 2687008 | tf_op jit(solution)/shard_map/all_to_all | solution.py:365
  53.9 3.4 %copy-done = bf16[128,2,1,128,128]{4,3,2,1,0:T(8,128)(2,1)S(1)} copy-done((bf16[128,2,1,128,128]{4,3,2,1,0:T(8,128)(2,1)S(1)}, bf16[128,2,1,128,128]{4,3,2,1,0:T(8,128)(2,1)}, u32[]{:S(2)}) %copy-start) | copy-done | bytes 8388632
  57.3 4.9 %attend.1 = bf16[16,32,1280]{2,1,0:T(8,128)(2,1)S(1)} custom-call(s32[640]{0:T(1024)S(1)} %pad_add_fusion.ints_ref, f32[16,328,128]{2,1,0:T(8,128)S(1)} %all-to-all-done.refs_0_, bf16[128,2,1,128,128]{4,3,2,1,0:T(8,128)(2,1)S(1)} %copy-done), custom_call_target="tpu_custom_call" | custom-call | flops 134217728 | bytes 10485760 | tf_op jit(solution)/shard_map/attend/pallas_call | solution.py:217
  63.3 3.7 %all-to-all-start.1 = ((bf16[16,32,1280]{2,1,0:T(8,128)(2,1)}), bf16[16,32,1280]{2,1,0:T(8,128)(2,1)S(1)}, u32[]{:S(2)}, u32[]{:S(2)}) async-start(bf16[16,32,1280]{2,1,0:T(8,128)(2,1)} %copy-done.4), calls=%async_computation.1 | async-start | bytes 2621440 | tf_op jit(solution)/shard_map/all_to_all | solution.py:365
  67.0 3.3 %gather_pages.3 = bf16[16,4,2,128,128]{4,3,2,1,0:T(8,128)(2,1)S(1)} custom-call(s32[640]{0:T(1024)S(1)} %pad_add_fusion.ints_ref, bf16[128,2,1,128,128]{4,3,2,1,0:T(8,128)(2,1)} %pool_ref.3), custom_call_target="tpu_custom_call" | custom-call | bytes 8388608 | tf_op jit(solution)/shard_map/gather_pages/pallas_call | solution.py:125
  70.3 2.0 copy-done.2
  72.4 14.3 %all-to-all-done.1.rows_ref = bf16[16,32,1280]{2,1,0:T(8,128)(2,1)S(1)} async-done(((bf16[16,32,1280]{2,1,0:T(8,128)(2,1)}), bf16[16,32,1280]{2,1,0:T(8,128)(2,1)S(1)}, u32[]{:S(2)}, u32[]{:S(2)}) %all-to-all-start.1) | async-done | bytes 1310752 | tf_op jit(solution)/shard_map/all_to_all | solution.py:365
  86.6 4.6 %all-to-all-start.3 = ((bf16[16,4,2,128,128]{4,3,2,1,0:T(8,128)(2,1)}), bf16[16,4,2,128,128]{4,3,2,1,0:T(8,128)(2,1)}, u32[]{:S(2)}, u32[]{:S(2)}) async-start(bf16[16,4,2,128,128]{4,3,2,1,0:T(8,128)(2,1)} %copy-done.2), calls=%async_computation.3 | async-start | bytes 8388608 | tf_op jit(solution)/shard_map/all_to_all | solution.py:365
  91.2 3.0 %gather_pages.2 = bf16[16,4,2,128,128]{4,3,2,1,0:T(8,128)(2,1)S(1)} custom-call(s32[640]{0:T(1024)S(1)} %pad_add_fusion.ints_ref, bf16[128,2,1,128,128]{4,3,2,1,0:T(8,128)(2,1)} %pool_ref.3), custom_call_target="tpu_custom_call" | custom-call | bytes 8388608 | tf_op jit(solution)/shard_map/gather_pages/pallas_call | solution.py:125
  94.2 2.0 copy-done.1
  96.2 51.0 %all-to-all-done.3.pages_ref = bf16[16,4,2,128,128]{4,3,2,1,0:T(8,128)(2,1)} async-done(((bf16[16,4,2,128,128]{4,3,2,1,0:T(8,128)(2,1)}), bf16[16,4,2,128,128]{4,3,2,1,0:T(8,128)(2,1)}, u32[]{:S(2)}, u32[]{:S(2)}) %all-to-all-start.3) | async-done | bytes 4194336 | tf_op jit(solution)/shard_map/all_to_all | solution.py:365
  147.2 4.5 %all-to-all-start.2 = ((bf16[16,4,2,128,128]{4,3,2,1,0:T(8,128)(2,1)}), bf16[16,4,2,128,128]{4,3,2,1,0:T(8,128)(2,1)}, u32[]{:S(2)}, u32[]{:S(2)}) async-start(bf16[16,4,2,128,128]{4,3,2,1,0:T(8,128)(2,1)} %copy-done.1), calls=%async_computation.2 | async-start | bytes 8388608 | tf_op jit(solution)/shard_map/all_to_all | solution.py:365
  151.8 1.6 output_rows.1
  154.1 1.9 collective-permute-start.1
  156.0 1.7 collective-permute-start.2
  157.7 2.0 collective-permute-start.3
  160.9 1.4 collective-permute-start.5
  163.5 1.4 collective-permute-done.2.refs_3_
  164.9 4.6 %collective-permute-done.3.refs_4_ = f32[64,512]{1,0:T(8,128)S(1)} collective-permute-done((f32[64,512]{1,0:T(8,128)S(1)}, f32[64,512]{1,0:T(8,128)S(1)}, u32[]{:S(2)}, u32[]{:S(2)}) %collective-permute-start.3) | collective-permute-done | bytes 131104 | tf_op jit(solution)/shard_map/ppermute | solution.py:43
  169.5 2.0 collective-permute-done.4.refs_5_
  172.8 2.0 total_rows.1.refs_0_
  174.8 2.6 %collective-permute-start.13 = (bf16[64,512]{1,0:T(8,128)(2,1)}, bf16[64,512]{1,0:T(8,128)(2,1)S(1)}, u32[]{:S(2)}, u32[]{:S(2)}) collective-permute-start(bf16[64,512]{1,0:T(8,128)(2,1)} %total_rows.1.refs_0_), channel_id=1, source_target_pairs={{0,7},{1,6},{2,1},{3,0},{4,3},{5,2},{6,5},{7,4},{8,15},{9,14},{10,... | collective-permute-start | bytes 196616 | tf_op jit(solution)/shard_map/ppermute | solution.py:43
  179.3 1.8 collective-permute-start.10
  182.7 1.6 collective-permute-done.11.refs_5_
  184.3 1.4 collective-permute-done.10.refs_4_
  186.4 2.3 %collective-permute-done.8.refs_2_ = bf16[64,512]{1,0:T(8,128)(2,1)S(1)} collective-permute-done((bf16[64,512]{1,0:T(8,128)(2,1)}, bf16[64,512]{1,0:T(8,128)(2,1)S(1)}, u32[]{:S(2)}, u32[]{:S(2)}) %collective-permute-start.8) | collective-permute-done | bytes 65568 | tf_op jit(solution)/shard_map/ppermute | solution.py:43
  190.0 1.9 order_rows.1
  191.9 5.7 %insert_tokens.2.refs_0_ = bf16[16,8,2,1,128,128]{5,4,3,2,1,0:T(8,128)(2,1)} custom-call(s32[640]{0:T(1024)S(1)} %pad_add_fusion.ints_ref, bf16[16,32,1280]{2,1,0:T(8,128)(2,1)S(1)} %all-to-all-done.1.rows_ref, bf16[16,4,2,128,128]{4,3,2,1,0:T(8,128)(2,1)} %all-to-all-done.3.pages_ref), custom_call_target="tpu_custom_call" | custom-call | bytes 8388608 | tf_op jit(solution)/shard_map/insert_tokens/pallas_call | solution.py:351
  197.5 11.6 %all-to-all-done.2.pages_ref = bf16[16,4,2,128,128]{4,3,2,1,0:T(8,128)(2,1)} async-done(((bf16[16,4,2,128,128]{4,3,2,1,0:T(8,128)(2,1)}), bf16[16,4,2,128,128]{4,3,2,1,0:T(8,128)(2,1)}, u32[]{:S(2)}, u32[]{:S(2)}) %all-to-all-start.2) | async-done | bytes 4194336 | tf_op jit(solution)/shard_map/all_to_all | solution.py:365
  209.1 5.2 %insert_tokens.3 = bf16[16,8,2,1,128,128]{5,4,3,2,1,0:T(8,128)(2,1)} custom-call(s32[640]{0:T(1024)S(1)} %pad_add_fusion.ints_ref, bf16[16,32,1280]{2,1,0:T(8,128)(2,1)S(1)} %all-to-all-done.1.rows_ref, bf16[16,4,2,128,128]{4,3,2,1,0:T(8,128)(2,1)} %all-to-all-done.2.pages_ref, ...), custom_call_target="tpu_custom_call", output_to_operand_aliasing={{}: (3, {})} | custom-call | bytes 8388608 | tf_op jit(solution)/shard_map/insert_tokens/pallas_call | solution.py:351
  (68 shorter events, 14.8 us)
Async XLA Ops:
  3.7 9.5 %copy-start.23 = (s32[16,16]{1,0:T(8,128)S(1)}, s32[16,16]{1,0:T(8,128)}, u32[]{:S(2)}) copy-start(s32[16,16]{1,0:T(8,128)} %param.9) | copy-start | bytes 3076
  3.7 9.6 %copy-start.24 = (s32[256]{0:T(256)S(1)}, s32[256]{0:T(256)}, u32[]{:S(2)}) copy-start(s32[256]{0:T(256)} %param.8) | copy-start | bytes 3076
  3.7 9.6 %copy-start.25 = (s32[1,128]{1,0:T(1,128)S(1)}, s32[1,128]{1,0:T(1,128)}, u32[]{:S(2)}) copy-start(s32[1,128]{1,0:T(1,128)} %param.10) | copy-start | bytes 1540
  6.1 47.8 %all-to-all-start = ((f32[16,328,128]{2,1,0:T(8,128)}), f32[16,328,128]{2,1,0:T(8,128)S(1)}, u32[]{:S(2)}, u32[]{:S(2)}) async-start(f32[16,328,128]{2,1,0:T(8,128)} %copy-done.3), calls=%async_computation | async-start | bytes 5373952 | tf_op jit(solution)/shard_map/all_to_all | solution.py:365
  53.9 3.4 %copy-start = (bf16[128,2,1,128,128]{4,3,2,1,0:T(8,128)(2,1)S(1)}, bf16[128,2,1,128,128]{4,3,2,1,0:T(8,128)(2,1)}, u32[]{:S(2)}) copy-start(bf16[128,2,1,128,128]{4,3,2,1,0:T(8,128)(2,1)} %pool_ref.3) | copy-start | bytes 25165828
  63.3 23.3 %all-to-all-start.1 = ((bf16[16,32,1280]{2,1,0:T(8,128)(2,1)}), bf16[16,32,1280]{2,1,0:T(8,128)(2,1)S(1)}, u32[]{:S(2)}, u32[]{:S(2)}) async-start(bf16[16,32,1280]{2,1,0:T(8,128)(2,1)} %copy-done.4), calls=%async_computation.1 | async-start | bytes 2621440 | tf_op jit(solution)/shard_map/all_to_all | solution.py:365
  86.6 60.6 %all-to-all-start.3 = ((bf16[16,4,2,128,128]{4,3,2,1,0:T(8,128)(2,1)}), bf16[16,4,2,128,128]{4,3,2,1,0:T(8,128)(2,1)}, u32[]{:S(2)}, u32[]{:S(2)}) async-start(bf16[16,4,2,128,128]{4,3,2,1,0:T(8,128)(2,1)} %copy-done.2), calls=%async_computation.3 | async-start | bytes 8388608 | tf_op jit(solution)/shard_map/all_to_all | solution.py:365
  96.2 55.5 %copy-start.6 = (bf16[1,1024,512]{2,1,0:T(8,128)(2,1)S(1)}, bf16[1,1024,512]{2,1,0:T(8,128)(2,1)}, u32[]{:S(2)}) copy-start(bf16[1,1024,512]{2,1,0:T(8,128)(2,1)} %param.15) | copy-start | bytes 3145732
  147.2 61.9 %all-to-all-start.2 = ((bf16[16,4,2,128,128]{4,3,2,1,0:T(8,128)(2,1)}), bf16[16,4,2,128,128]{4,3,2,1,0:T(8,128)(2,1)}, u32[]{:S(2)}, u32[]{:S(2)}) async-start(bf16[16,4,2,128,128]{4,3,2,1,0:T(8,128)(2,1)} %copy-done.1), calls=%async_computation.2 | async-start | bytes 8388608 | tf_op jit(solution)/shard_map/all_to_all | solution.py:365
  154.1 6.8 %collective-permute-start = (f32[64,512]{1,0:T(8,128)S(1)}, f32[64,512]{1,0:T(8,128)S(1)}, u32[]{:S(2)}, u32[]{:S(2)}) collective-permute-start(f32[64,512]{1,0:T(8,128)S(1)} %get-tuple-element.13), channel_id=1, source_target_pairs={{0,1},{1,0},{2,3},{3,2},{4,5},{5,4},{6,7},{7,6},{8,9},{9,8},{10,11... | collective-permute-start | bytes 393224 | tf_op jit(solution)/shard_map/ppermute | solution.py:43
  154.1 8.4 %collective-permute-start.1 = (f32[64,512]{1,0:T(8,128)S(1)}, f32[64,512]{1,0:T(8,128)S(1)}, u32[]{:S(2)}, u32[]{:S(2)}) collective-permute-start(f32[64,512]{1,0:T(8,128)S(1)} %get-tuple-element.14), channel_id=1, source_target_pairs={{0,2},{1,3},{2,4},{3,5},{4,6},{5,7},{6,0},{7,1},{8,10},{9,11},{10,... | collective-permute-start | bytes 393224 | tf_op jit(solution)/shard_map/ppermute | solution.py:43
  156.0 8.9 %collective-permute-start.2 = (f32[64,512]{1,0:T(8,128)S(1)}, f32[64,512]{1,0:T(8,128)S(1)}, u32[]{:S(2)}, u32[]{:S(2)}) collective-permute-start(f32[64,512]{1,0:T(8,128)S(1)} %get-tuple-element.15), channel_id=1, source_target_pairs={{0,3},{1,2},{2,5},{3,4},{4,7},{5,6},{6,1},{7,0},{8,11},{9,10},{10,... | collective-permute-start | bytes 393224 | tf_op jit(solution)/shard_map/ppermute | solution.py:43
  157.7 11.7 %collective-permute-start.3 = (f32[64,512]{1,0:T(8,128)S(1)}, f32[64,512]{1,0:T(8,128)S(1)}, u32[]{:S(2)}, u32[]{:S(2)}) collective-permute-start(f32[64,512]{1,0:T(8,128)S(1)} %get-tuple-element.16), channel_id=1, source_target_pairs={{0,4},{1,5},{2,6},{3,7},{4,0},{5,1},{6,2},{7,3},{8,12},{9,13},{10,... | collective-permute-start | bytes 393224 | tf_op jit(solution)/shard_map/ppermute | solution.py:43
  159.7 11.8 %collective-permute-start.4 = (f32[64,512]{1,0:T(8,128)S(1)}, f32[64,512]{1,0:T(8,128)S(1)}, u32[]{:S(2)}, u32[]{:S(2)}) collective-permute-start(f32[64,512]{1,0:T(8,128)S(1)} %get-tuple-element.17), channel_id=1, source_target_pairs={{0,5},{1,4},{2,7},{3,6},{4,1},{5,0},{6,3},{7,2},{8,13},{9,12},{10,... | collective-permute-start | bytes 393224 | tf_op jit(solution)/shard_map/ppermute | solution.py:43
  160.9 11.3 %copy-start.9 = (f32[64,512]{1,0:T(8,128)}, f32[64,512]{1,0:T(8,128)S(1)}, u32[]{:S(2)}) copy-start(f32[64,512]{1,0:T(8,128)S(1)} %collective-permute-done.refs_1_) | copy-start | bytes 393220
  160.9 10.6 %collective-permute-start.5 = (f32[64,512]{1,0:T(8,128)S(1)}, f32[64,512]{1,0:T(8,128)S(1)}, u32[]{:S(2)}, u32[]{:S(2)}) collective-permute-start(f32[64,512]{1,0:T(8,128)S(1)} %get-tuple-element.18), channel_id=1, source_target_pairs={{0,6},{1,7},{2,0},{3,1},{4,2},{5,3},{6,4},{7,5},{8,14},{9,15},{10,... | collective-permute-start | bytes 393224 | tf_op jit(solution)/shard_map/ppermute | solution.py:43
  162.5 9.7 %copy-start.10 = (f32[64,512]{1,0:T(8,128)}, f32[64,512]{1,0:T(8,128)S(1)}, u32[]{:S(2)}) copy-start(f32[64,512]{1,0:T(8,128)S(1)} %collective-permute-done.1.refs_2_) | copy-start | bytes 393220
  162.5 9.7 %collective-permute-start.6 = (f32[64,512]{1,0:T(8,128)S(1)}, f32[64,512]{1,0:T(8,128)S(1)}, u32[]{:S(2)}, u32[]{:S(2)}) collective-permute-start(f32[64,512]{1,0:T(8,128)S(1)} %get-tuple-element.19), channel_id=1, source_target_pairs={{0,7},{1,6},{2,1},{3,0},{4,3},{5,2},{6,5},{7,4},{8,15},{9,14},{10,... | collective-permute-start | bytes 393224 | tf_op jit(solution)/shard_map/ppermute | solution.py:43
  164.9 7.3 %copy-start.11 = (f32[64,512]{1,0:T(8,128)}, f32[64,512]{1,0:T(8,128)S(1)}, u32[]{:S(2)}) copy-start(f32[64,512]{1,0:T(8,128)S(1)} %collective-permute-done.2.refs_3_) | copy-start | bytes 393220
  169.5 2.7 %copy-start.12 = (f32[64,512]{1,0:T(8,128)}, f32[64,512]{1,0:T(8,128)S(1)}, u32[]{:S(2)}) copy-start(f32[64,512]{1,0:T(8,128)S(1)} %collective-permute-done.3.refs_4_) | copy-start | bytes 393220
  174.8 7.6 %collective-permute-start.13 = (bf16[64,512]{1,0:T(8,128)(2,1)}, bf16[64,512]{1,0:T(8,128)(2,1)S(1)}, u32[]{:S(2)}, u32[]{:S(2)}) collective-permute-start(bf16[64,512]{1,0:T(8,128)(2,1)} %total_rows.1.refs_0_), channel_id=1, source_target_pairs={{0,7},{1,6},{2,1},{3,0},{4,3},{5,2},{6,5},{7,4},{8,15},{9,14},{10,... | collective-permute-start | bytes 196616 | tf_op jit(solution)/shard_map/ppermute | solution.py:43
  177.4 5.2 %collective-permute-start.12 = (bf16[64,512]{1,0:T(8,128)(2,1)}, bf16[64,512]{1,0:T(8,128)(2,1)S(1)}, u32[]{:S(2)}, u32[]{:S(2)}) collective-permute-start(bf16[64,512]{1,0:T(8,128)(2,1)} %total_rows.1.refs_0_), channel_id=1, source_target_pairs={{0,6},{1,7},{2,0},{3,1},{4,2},{5,3},{6,4},{7,5},{8,14},{9,15},{10,... | collective-permute-start | bytes 196616 | tf_op jit(solution)/shard_map/ppermute | solution.py:43
  178.6 5.7 %collective-permute-start.11 = (bf16[64,512]{1,0:T(8,128)(2,1)}, bf16[64,512]{1,0:T(8,128)(2,1)S(1)}, u32[]{:S(2)}, u32[]{:S(2)}) collective-permute-start(bf16[64,512]{1,0:T(8,128)(2,1)} %total_rows.1.refs_0_), channel_id=1, source_target_pairs={{0,5},{1,4},{2,7},{3,6},{4,1},{5,0},{6,3},{7,2},{8,13},{9,12},{10,... | collective-permute-start | bytes 196616 | tf_op jit(solution)/shard_map/ppermute | solution.py:43
  179.3 6.4 %collective-permute-start.10 = (bf16[64,512]{1,0:T(8,128)(2,1)}, bf16[64,512]{1,0:T(8,128)(2,1)S(1)}, u32[]{:S(2)}, u32[]{:S(2)}) collective-permute-start(bf16[64,512]{1,0:T(8,128)(2,1)} %total_rows.1.refs_0_), channel_id=1, source_target_pairs={{0,4},{1,5},{2,6},{3,7},{4,0},{5,1},{6,2},{7,3},{8,12},{9,13},{10,... | collective-permute-start | bytes 196616 | tf_op jit(solution)/shard_map/ppermute | solution.py:43
  181.1 5.3 %collective-permute-start.9 = (bf16[64,512]{1,0:T(8,128)(2,1)}, bf16[64,512]{1,0:T(8,128)(2,1)S(1)}, u32[]{:S(2)}, u32[]{:S(2)}) collective-permute-start(bf16[64,512]{1,0:T(8,128)(2,1)} %total_rows.1.refs_0_), channel_id=1, source_target_pairs={{0,3},{1,2},{2,5},{3,4},{4,7},{5,6},{6,1},{7,0},{8,11},{9,10},{10,... | collective-permute-start | bytes 196616 | tf_op jit(solution)/shard_map/ppermute | solution.py:43
  182.4 6.3 %copy-start.16 = (bf16[64,512]{1,0:T(8,128)(2,1)}, bf16[64,512]{1,0:T(8,128)(2,1)S(1)}, u32[]{:S(2)}) copy-start(bf16[64,512]{1,0:T(8,128)(2,1)S(1)} %collective-permute-done.13.refs_7_) | copy-start | bytes 196612
  182.4 6.3 %collective-permute-start.8 = (bf16[64,512]{1,0:T(8,128)(2,1)}, bf16[64,512]{1,0:T(8,128)(2,1)S(1)}, u32[]{:S(2)}, u32[]{:S(2)}) collective-permute-start(bf16[64,512]{1,0:T(8,128)(2,1)} %total_rows.1.refs_0_), channel_id=1, source_target_pairs={{0,2},{1,3},{2,4},{3,5},{4,6},{5,7},{6,0},{7,1},{8,10},{9,11},{10,... | collective-permute-start | bytes 196616 | tf_op jit(solution)/shard_map/ppermute | solution.py:43
  182.6 6.1 %copy-start.17 = (bf16[64,512]{1,0:T(8,128)(2,1)}, bf16[64,512]{1,0:T(8,128)(2,1)S(1)}, u32[]{:S(2)}) copy-start(bf16[64,512]{1,0:T(8,128)(2,1)S(1)} %collective-permute-done.12.refs_6_) | copy-start | bytes 196612
  182.6 6.1 %collective-permute-start.7 = (bf16[64,512]{1,0:T(8,128)(2,1)}, bf16[64,512]{1,0:T(8,128)(2,1)S(1)}, u32[]{:S(2)}, u32[]{:S(2)}) collective-permute-start(bf16[64,512]{1,0:T(8,128)(2,1)} %total_rows.1.refs_0_), channel_id=1, source_target_pairs={{0,1},{1,0},{2,3},{3,2},{4,5},{5,4},{6,7},{7,6},{8,9},{9,8},{10,11... | collective-permute-start | bytes 196616 | tf_op jit(solution)/shard_map/ppermute | solution.py:43
  184.3 4.4 %copy-start.18 = (bf16[64,512]{1,0:T(8,128)(2,1)}, bf16[64,512]{1,0:T(8,128)(2,1)S(1)}, u32[]{:S(2)}) copy-start(bf16[64,512]{1,0:T(8,128)(2,1)S(1)} %collective-permute-done.11.refs_5_) | copy-start | bytes 196612
  185.7 3.0 %copy-start.19 = (bf16[64,512]{1,0:T(8,128)(2,1)}, bf16[64,512]{1,0:T(8,128)(2,1)S(1)}, u32[]{:S(2)}) copy-start(bf16[64,512]{1,0:T(8,128)(2,1)S(1)} %collective-permute-done.10.refs_4_) | copy-start | bytes 196612
  186.4 2.3 %copy-start.20 = (bf16[64,512]{1,0:T(8,128)(2,1)}, bf16[64,512]{1,0:T(8,128)(2,1)S(1)}, u32[]{:S(2)}) copy-start(bf16[64,512]{1,0:T(8,128)(2,1)S(1)} %collective-permute-done.9.refs_3_) | copy-start | bytes 196612
  (12 other events, 13.0 us)

commit v2 on v1

--- a/solution.py
+++ b/solution.py
@@ -135,7 +135,7 @@
 
 
 def attend_kernel(ints_ref, *refs):
-    sums_ref, pool_ref, out_ref, proj, done = refs
+    sums_ref, pool_ref, out_ref, new_ref, proj, done = refs
     me = lax.axis_index("grp")
     step = pl.program_id(0)
     block = SLOTS // pl.num_programs(0)
@@ -208,20 +208,23 @@
             part = source[c * ROWS:(c + 1) * ROWS, :].astype(out_ref.dtype)
             for g in range(out_ref.shape[0]):
                 out_ref[g, :, c * HD:(c + 1) * HD] = part
+        for kv in range(2):
+            new_ref[kv] = proj[(heads + kv) * ROWS:(heads + kv + 1) * ROWS, :]
 
 
 def attend(ints, sums, pool):
     blocks = sums.shape[1] // ROWS
     whole = lambda a: pl.BlockSpec(a.shape, lambda i, *_: (0,) * len(a.shape))
     out = jax.ShapeDtypeStruct((sums.shape[0], ROWS, blocks * HD), jnp.bfloat16)
+    new = jax.ShapeDtypeStruct((2, ROWS, HD), jnp.float32)
     return pl.pallas_call(
         attend_kernel,
-        out_shape=out,
+        out_shape=(out, new),
         grid_spec=pltpu.PrefetchScalarGridSpec(
             num_scalar_prefetch=1,
             grid=(4,),
             in_specs=[VMEM, VMEM],
-            out_specs=whole(out),
+            out_specs=(whole(out), whole(new)),
             scratch_shapes=[pltpu.VMEM((blocks * ROWS, HD), jnp.float32), pltpu.VMEM(((blocks - 2) * ROWS, HD), jnp.float32)],
         ),
         compiler_params=params(24),
@@ -346,19 +349,114 @@
         store.wait()
 
 
-def insert(low, ints, rows, pages, cache):
-    before = [] if cache is None else [cache]
+def insert(low, ints, rows, pages):
     return pl.pallas_call(
         functools.partial(insert_kernel, low),
         out_shape=jax.ShapeDtypeStruct((SLOTS, MAXP, 2, 1, PAGE, HD), pages.dtype),
-        in_specs=[SMEM, VMEM, ANY] + [ANY] * len(before),
+        in_specs=[SMEM, VMEM, ANY],
         out_specs=ANY,
         scratch_shapes=[pltpu.VMEM(pages.shape, pages.dtype), pltpu.SemaphoreType.DMA((2, SLOTS))],
-        input_output_aliases={3: 0} if before else {},
         compiler_params=params(44),
         cost_estimate=cost(0, 2 * pages.size * 2),
         name="insert_tokens",
-    )(ints, rows, pages, *before)
+    )(ints, rows, pages)
+
+
+def write_kernel(low, ints_ref, new_ref, pages_in, pages_ref, box, sems):
+    count = pages_ref.shape[1]
+    me = lax.axis_index("grp")
+
+    def spot(j, which):
+        at = ints_ref[LENGTH + me * SLOTS + j]
+        base = (at // TILE) * TILE + which * TILE
+        return at, base
+
+    def view(j, which):
+        _, base = spot(j, which)
+        page = base // PAGE
+        row = pl.multiple_of(base - page * PAGE, TILE)
+        return pages_ref.at[ints_ref[OWNER + me * SLOTS + j], page - low, :, pl.ds(row, TILE)]
+
+    def load(j, which):
+        return pltpu.make_async_copy(view(j, which), box.at[j, which], sems.at[0, j, which])
+
+    def store(j, which):
+        return pltpu.make_async_copy(box.at[j, which], view(j, which), sems.at[1, j, which])
+
+    def each(act):
+        def body(j, carry):
+            at, base = spot(j, 0)
+
+            def held(base):
+                return (base >= low * PAGE) & (base < (low + count) * PAGE)
+
+            @pl.when(held(base))
+            def _():
+                act(j, 0)
+
+            @pl.when((at + STEPS > base + TILE) & held(base + TILE))
+            def _():
+                act(j, 1)
+            return carry
+        lax.fori_loop(0, SLOTS, body, 0)
+
+    tile_rows = lax.broadcasted_iota(jnp.int32, (TILE, HD), 0)
+
+    def fill(j, which):
+        load(j, which).wait()
+        at, base = spot(j, which)
+        for kv in range(2):
+            tile = box[j, which, kv].astype(jnp.float32)
+            for s in range(STEPS):
+                token = jnp.broadcast_to(new_ref[kv, pl.ds(s * SLOTS + j, 1), :], (TILE, HD))
+                tile = jnp.where(tile_rows == at + s - base, token, tile)
+            box[j, which, kv] = tile.astype(box.dtype)
+        store(j, which).start()
+
+    each(lambda j, which: load(j, which).start())
+    each(fill)
+    each(lambda j, which: store(j, which).wait())
+
+
+def write_tokens(low, ints, new, pages):
+    return pl.pallas_call(
+        functools.partial(write_kernel, low),
+        out_shape=jax.ShapeDtypeStruct(pages.shape, pages.dtype),
+        in_specs=[SMEM, VMEM, ANY],
+        out_specs=ANY,
+        scratch_shapes=[pltpu.VMEM((SLOTS, 2, 2, TILE, HD), pages.dtype), pltpu.SemaphoreType.DMA((2, SLOTS, 2))],
+        input_output_aliases={2: 0},
+        compiler_params=params(54),
+        cost_estimate=cost(0, 2**20),
+        name="write_tokens",
+    )(ints, new, pages)
+
+
+def settle_kernel(low, pages_ref, cache_in, cache_ref, box, sems):
+    count = pages_ref.shape[1]
+    loads = [pltpu.make_async_copy(pages_ref.at[r], box.at[r], sems.at[0, r]) for r in range(SLOTS)]
+    stores = [pltpu.make_async_copy(box.at[r], cache_ref.at[r, pl.ds(low, count), :, 0], sems.at[1, r]) for r in range(SLOTS)]
+    for load in loads:
+        load.start()
+    for load, store in zip(loads, stores):
+        load.wait()
+        store.start()
+    for store in stores:
+        store.wait()
+
+
+def settle(low, pages, cache):
+    return pl.pallas_call(
+        functools.partial(settle_kernel, low),
+        out_shape=jax.ShapeDtypeStruct(cache.shape, cache.dtype),
+        in_specs=[ANY, ANY],
+        out_specs=ANY,
+        scratch_shapes=[pltpu.VMEM(pages.shape, pages.dtype), pltpu.SemaphoreType.DMA((2, SLOTS))],
+        input_output_aliases={1: 0},
+        compiler_params=params(44),
+        cost_estimate=cost(0, 2 * pages.size * 2),
+        name="settle",
+    )(pages, cache)
 
 
 def exchange(array):
@@ -372,19 +470,20 @@
     ints = jnp.concatenate([request_owner.reshape(-1), prompt_len, page_table.reshape(-1)])
 
     partial = project(step_input, norm_gain.reshape(1, width), w_qkv.reshape(width, blocks * HD), request_owner.shape[0])
-    pages = [gather_pages(low, high, ints, kv_pool) for low, high in zip(CUTS, CUTS[1:])]
-    mine = attend(ints, exchange(partial), kv_pool)
-    rows = exchange(mine)
-    received = [exchange(lax.optimization_barrier((piece, rows))[0]) for piece in pages]
+    near, far = [gather_pages(low, high, ints, kv_pool) for low, high in zip(CUTS, CUTS[1:])]
+    sums = exchange(partial)
+    near = exchange(lax.optimization_barrier((near, sums))[0])
+    mine, new = attend(ints, sums, kv_pool)
+    far = write_tokens(CUTS[1], ints, new, far)
+    rows = exchange(lax.optimization_barrier((mine, near))[0])
+    far = exchange(lax.optimization_barrier((far, rows))[0])
 
     parts = output_rows(rows, w_out.reshape(heads * HD, width))
     distances = [divmod(i, CORES) for i in range(SIDE * CORES)]
     own = total_rows([parts[0]] + [move_part(parts[i], *distances[i]) for i in range(1, len(parts))])
     attn_out = order_rows([own] + [move_part(own, *d) for d in distances[1:]])
 
-    cache = None
-    for low, piece in zip(CUTS, received):
-        cache = insert(low, ints, rows, piece, cache)
+    cache = settle(CUTS[1], far, insert(CUTS[0], ints, rows, near))
     return (attn_out, cache)
 
 

time: 215 us -> 205 us (0.953)
  waiting for transfers between devices: 132 us -> 119 us
  Pallas kernels: 28.4 us -> 30.7 us
    all_to_all x4, waiting for transfers between devices: 117 us -> 110 us  [exchange(): return lax.all_to_all(array, 'grp', split_axis=0, concat_axis=0, tiled=True)]
    pallas_call x1 -> x3, Pallas kernels: 4.92 us -> 12.2 us  [the longest x1 4.92 us: attend(): pl.pallas_call(attend_kernel, out_shape=(out, new), grid_spec=pltpu.Prefe...]
    ppermute x14, waiting for transfers between devices: 14.9 us -> 9.18 us  [move_part(): return lax.ppermute(array, 'tp', pairs)]
    pallas_call x2 -> x1, Pallas kernels: 10.9 us -> 5.67 us  [insert(): pl.pallas_call(functools.partial(insert_kernel, low), out_shape=jax.Shape...]
    unnamed x52 -> x58, local copies, waits for them, and re-layouts: 14.9 us -> 15.5 us
  transfers between devices with their start and end apart: 18 -> 18, of which waited for: 13 -> 10; matrix products, arithmetic and copies ran while one was open for 0% -> 0% of each run, Pallas kernels for 8% -> 13%
where the time goes in v2:
time: 205 us; the launch traced here: 204 us
  waiting for transfers between devices  119 us (58%)
  starting transfers between devices  37.7 us (18%)
  Pallas kernels  30.7 us (15%)
  local copies, waits for them, and re-layouts  16.3 us (8%)
    all_to_all x4, waiting for transfers between devices, exchange(): return lax.all_to_all(array, 'grp', split_axis=0, concat_axis=0, tiled=True)  110 us
    all_to_all x4, starting transfers between devices, exchange(): return lax.all_to_all(array, 'grp', split_axis=0, concat_axis=0, tiled=True)  20.7 us
    ppermute x14, starting transfers between devices, move_part(): return lax.ppermute(array, 'tp', pairs)  17 us
    unnamed x58, local copies, waits for them, and re-layouts  15.5 us
    ppermute x14, waiting for transfers between devices, move_part(): return lax.ppermute(array, 'tp', pairs)  9.18 us
    pallas_call x2, Pallas kernels, gather_pages(): pl.pallas_call(functools.partial(gather_kernel, low), out_shape=shape, in...  6.46 us
    pallas_call x1, Pallas kernels, insert(): pl.pallas_call(functools.partial(insert_kernel, low), out_shape=jax.Shape...  5.67 us
    pallas_call x1, Pallas kernels, attend(): pl.pallas_call(attend_kernel, out_shape=(out, new), grid_spec=pltpu.Prefe...  4.92 us
  transfers between devices with their start and end apart: 18, of which 10 were waited for; matrix products, arithmetic and copies ran while one was open for 0% of the time, Pallas kernels for 13%

profile of v2, /device:TPU:0, one launch (start us, length us, event | category | flops | bytes accessed | tf_op | source)
XLA Modules:
  0.0 204.4 jit_solution(7934510418153499901)
XLA Ops:
  1.3 1.3 copy-done.5
  4.5 1.5 copy-done.3
  6.0 7.1 %all-to-all-start = ((f32[16,328,128]{2,1,0:T(8,128)}), f32[16,328,128]{2,1,0:T(8,128)S(1)}, u32[]{:S(2)}, u32[]{:S(2)}) async-start(f32[16,328,128]{2,1,0:T(8,128)} %copy-done.3), calls=%async_computation | async-start | bytes 5373952 | tf_op jit(solution)/shard_map/all_to_all | solution.py:463
  13.3 3.3 %gather_pages.2 = bf16[16,4,2,128,128]{4,3,2,1,0:T(8,128)(2,1)S(1)} custom-call(s32[640]{0:T(1024)S(1)} %pad_add_fusion.ints_ref, bf16[128,2,1,128,128]{4,3,2,1,0:T(8,128)(2,1)} %pool_ref.3), custom_call_target="tpu_custom_call" | custom-call | bytes 8388608 | tf_op jit(solution)/shard_map/gather_pages/pallas_call | solution.py:125
  16.6 2.0 copy-done.2
  18.6 35.3 %all-to-all-done.refs_0_ = f32[16,328,128]{2,1,0:T(8,128)S(1)} async-done(((f32[16,328,128]{2,1,0:T(8,128)}), f32[16,328,128]{2,1,0:T(8,128)S(1)}, u32[]{:S(2)}, u32[]{:S(2)}) %all-to-all-start) | async-done | bytes 2687008 | tf_op jit(solution)/shard_map/all_to_all | solution.py:463
  53.9 4.6 %all-to-all-start.1 = ((bf16[16,4,2,128,128]{4,3,2,1,0:T(8,128)(2,1)}), bf16[16,4,2,128,128]{4,3,2,1,0:T(8,128)(2,1)}, u32[]{:S(2)}, u32[]{:S(2)}) async-start(bf16[16,4,2,128,128]{4,3,2,1,0:T(8,128)(2,1)} %copy-done.2), calls=%async_computation.1 | async-start | bytes 8388608 | tf_op jit(solution)/shard_map/all_to_all | solution.py:463
  58.5 3.4 %copy-done = bf16[128,2,1,128,128]{4,3,2,1,0:T(8,128)(2,1)S(1)} copy-done((bf16[128,2,1,128,128]{4,3,2,1,0:T(8,128)(2,1)S(1)}, bf16[128,2,1,128,128]{4,3,2,1,0:T(8,128)(2,1)}, u32[]{:S(2)}) %copy-start) | copy-done | bytes 8388632
  61.8 4.9 %attend.1 = (bf16[16,32,1280]{2,1,0:T(8,128)(2,1)S(1)}, f32[2,32,128]{2,1,0:T(8,128)S(1)}) custom-call(s32[640]{0:T(1024)S(1)} %pad_add_fusion.ints_ref, f32[16,328,128]{2,1,0:T(8,128)S(1)} %all-to-all-done.refs_0_, bf16[128,2,1,128,128]{4,3,2,1,0:T(8,128)(2,1)S(1)} %copy-done), custom_call_target="tpu_custom_call" | custom-call | flops 134217728 | bytes 10485760 | tf_op jit(solution)/shard_map/attend/pallas_call | solution.py:220
  68.5 50.6 %all-to-all-done.1.pages_ref = bf16[16,4,2,128,128]{4,3,2,1,0:T(8,128)(2,1)} async-done(((bf16[16,4,2,128,128]{4,3,2,1,0:T(8,128)(2,1)}), bf16[16,4,2,128,128]{4,3,2,1,0:T(8,128)(2,1)}, u32[]{:S(2)}, u32[]{:S(2)}) %all-to-all-start.1) | async-done | bytes 4194336 | tf_op jit(solution)/shard_map/all_to_all | solution.py:463
  119.1 4.4 %all-to-all-start.2 = ((bf16[16,32,1280]{2,1,0:T(8,128)(2,1)}), bf16[16,32,1280]{2,1,0:T(8,128)(2,1)S(1)}, u32[]{:S(2)}, u32[]{:S(2)}) async-start(bf16[16,32,1280]{2,1,0:T(8,128)(2,1)} %copy-done.4), calls=%async_computation.2 | async-start | bytes 2621440 | tf_op jit(solution)/shard_map/all_to_all | solution.py:463
  123.6 3.2 %gather_pages.3.pages_in = bf16[16,4,2,128,128]{4,3,2,1,0:T(8,128)(2,1)S(1)} custom-call(s32[640]{0:T(1024)S(1)} %pad_add_fusion.ints_ref, bf16[128,2,1,128,128]{4,3,2,1,0:T(8,128)(2,1)} %pool_ref.3), custom_call_target="tpu_custom_call" | custom-call | bytes 8388608 | tf_op jit(solution)/shard_map/gather_pages/pallas_call | solution.py:125
  126.8 2.0 copy-done.1
  128.8 3.4 %write_tokens.1 = bf16[16,4,2,128,128]{4,3,2,1,0:T(8,128)(2,1)} custom-call(s32[640]{0:T(1024)} %copy-done.8, f32[2,32,128]{2,1,0:T(8,128)} %copy-done.11, bf16[16,4,2,128,128]{4,3,2,1,0:T(8,128)(2,1)} %copy-done.1), custom_call_target="tpu_custom_call", output_to_operand_aliasing={{}: (2, {})} | custom-call | bytes 1048576 | tf_op jit(solution)/shard_map/write_tokens/pallas_call | solution.py:422
  132.2 10.0 %all-to-all-done.2.rows_ref = bf16[16,32,1280]{2,1,0:T(8,128)(2,1)S(1)} async-done(((bf16[16,32,1280]{2,1,0:T(8,128)(2,1)}), bf16[16,32,1280]{2,1,0:T(8,128)(2,1)S(1)}, u32[]{:S(2)}, u32[]{:S(2)}) %all-to-all-start.2) | async-done | bytes 1310752 | tf_op jit(solution)/shard_map/all_to_all | solution.py:463
  142.2 4.5 %all-to-all-start.3 = ((bf16[16,4,2,128,128]{4,3,2,1,0:T(8,128)(2,1)}), bf16[16,4,2,128,128]{4,3,2,1,0:T(8,128)(2,1)}, u32[]{:S(2)}, u32[]{:S(2)}) async-start(bf16[16,4,2,128,128]{4,3,2,1,0:T(8,128)(2,1)} %write_tokens.1), calls=%async_computation.3 | async-start | bytes 8388608 | tf_op jit(solution)/shard_map/all_to_all | solution.py:463
  146.8 1.6 output_rows.1
  149.1 1.9 collective-permute-start.1
  151.0 1.8 collective-permute-start.2
  152.8 1.9 collective-permute-start.3
  155.9 1.3 collective-permute-start.5
  158.5 1.4 collective-permute-done.2.refs_3_
  159.9 4.6 %collective-permute-done.3.refs_4_ = f32[64,512]{1,0:T(8,128)S(1)} collective-permute-done((f32[64,512]{1,0:T(8,128)S(1)}, f32[64,512]{1,0:T(8,128)S(1)}, u32[]{:S(2)}, u32[]{:S(2)}) %collective-permute-start.3) | collective-permute-done | bytes 131104 | tf_op jit(solution)/shard_map/ppermute | solution.py:43
  164.5 2.0 collective-permute-done.4.refs_5_
  167.8 2.0 total_rows.1.refs_0_
  169.8 2.6 %collective-permute-start.13 = (bf16[64,512]{1,0:T(8,128)(2,1)}, bf16[64,512]{1,0:T(8,128)(2,1)S(1)}, u32[]{:S(2)}, u32[]{:S(2)}) collective-permute-start(bf16[64,512]{1,0:T(8,128)(2,1)} %total_rows.1.refs_0_), channel_id=1, source_target_pairs={{0,7},{1,6},{2,1},{3,0},{4,3},{5,2},{6,5},{7,4},{8,15},{9,14},{10,... | collective-permute-start | bytes 196616 | tf_op jit(solution)/shard_map/ppermute | solution.py:43
  172.4 1.3 collective-permute-start.12
  174.3 1.8 collective-permute-start.10
  177.7 5.7 %insert_tokens.1.cache_in = bf16[16,8,2,1,128,128]{5,4,3,2,1,0:T(8,128)(2,1)} custom-call(s32[640]{0:T(1024)S(1)} %copy-done.9, bf16[16,32,1280]{2,1,0:T(8,128)(2,1)S(1)} %all-to-all-done.2.rows_ref, bf16[16,4,2,128,128]{4,3,2,1,0:T(8,128)(2,1)} %all-to-all-done.1.pages_ref), custom_call_target="tpu_custom_call" | custom-call | bytes 8388608 | tf_op jit(solution)/shard_map/insert_tokens/pallas_call | solution.py:353
  184.9 1.9 order_rows.1
  186.8 13.7 %all-to-all-done.3.pages_ref = bf16[16,4,2,128,128]{4,3,2,1,0:T(8,128)(2,1)} async-done(((bf16[16,4,2,128,128]{4,3,2,1,0:T(8,128)(2,1)}), bf16[16,4,2,128,128]{4,3,2,1,0:T(8,128)(2,1)}, u32[]{:S(2)}, u32[]{:S(2)}) %all-to-all-start.3) | async-done | bytes 4194336 | tf_op jit(solution)/shard_map/all_to_all | solution.py:463
  200.5 3.8 %settle.1 = bf16[16,8,2,1,128,128]{5,4,3,2,1,0:T(8,128)(2,1)} custom-call(bf16[16,4,2,128,128]{4,3,2,1,0:T(8,128)(2,1)} %all-to-all-done.3.pages_ref, bf16[16,8,2,1,128,128]{5,4,3,2,1,0:T(8,128)(2,1)} %insert_tokens.1.cache_in), custom_call_target="tpu_custom_call", output_to_operand_aliasing={{}: (1, {})} | custom-call | bytes 8388608 | tf_op jit(solution)/shard_map/settle/pallas_call | solution.py:449
  (75 shorter events, 12.5 us)
Async XLA Ops:
  3.7 9.5 %copy-start.26 = (s32[16,16]{1,0:T(8,128)S(1)}, s32[16,16]{1,0:T(8,128)}, u32[]{:S(2)}) copy-start(s32[16,16]{1,0:T(8,128)} %param.9) | copy-start | bytes 3076
  3.7 9.6 %copy-start.27 = (s32[256]{0:T(256)S(1)}, s32[256]{0:T(256)}, u32[]{:S(2)}) copy-start(s32[256]{0:T(256)} %param.8) | copy-start | bytes 3076
  3.7 9.6 %copy-start.28 = (s32[1,128]{1,0:T(1,128)S(1)}, s32[1,128]{1,0:T(1,128)}, u32[]{:S(2)}) copy-start(s32[1,128]{1,0:T(1,128)} %param.10) | copy-start | bytes 1540
  6.0 47.8 %all-to-all-start = ((f32[16,328,128]{2,1,0:T(8,128)}), f32[16,328,128]{2,1,0:T(8,128)S(1)}, u32[]{:S(2)}, u32[]{:S(2)}) async-start(f32[16,328,128]{2,1,0:T(8,128)} %copy-done.3), calls=%async_computation | async-start | bytes 5373952 | tf_op jit(solution)/shard_map/all_to_all | solution.py:463
  13.3 110.3 %copy-start.8 = (s32[640]{0:T(1024)}, s32[640]{0:T(1024)S(1)}, u32[]{:S(2)}) copy-start(s32[640]{0:T(1024)S(1)} %pad_add_fusion.ints_ref) | copy-start | bytes 7684
  53.9 65.2 %all-to-all-start.1 = ((bf16[16,4,2,128,128]{4,3,2,1,0:T(8,128)(2,1)}), bf16[16,4,2,128,128]{4,3,2,1,0:T(8,128)(2,1)}, u32[]{:S(2)}, u32[]{:S(2)}) async-start(bf16[16,4,2,128,128]{4,3,2,1,0:T(8,128)(2,1)} %copy-done.2), calls=%async_computation.1 | async-start | bytes 8388608 | tf_op jit(solution)/shard_map/all_to_all | solution.py:463
  58.4 3.4 %copy-start = (bf16[128,2,1,128,128]{4,3,2,1,0:T(8,128)(2,1)S(1)}, bf16[128,2,1,128,128]{4,3,2,1,0:T(8,128)(2,1)}, u32[]{:S(2)}) copy-start(bf16[128,2,1,128,128]{4,3,2,1,0:T(8,128)(2,1)} %pool_ref.3) | copy-start | bytes 25165828
  119.1 23.1 %all-to-all-start.2 = ((bf16[16,32,1280]{2,1,0:T(8,128)(2,1)}), bf16[16,32,1280]{2,1,0:T(8,128)(2,1)S(1)}, u32[]{:S(2)}, u32[]{:S(2)}) async-start(bf16[16,32,1280]{2,1,0:T(8,128)(2,1)} %copy-done.4), calls=%async_computation.2 | async-start | bytes 2621440 | tf_op jit(solution)/shard_map/all_to_all | solution.py:463
  126.8 2.1 %copy-start.1 = (bf16[16,4,2,128,128]{4,3,2,1,0:T(8,128)(2,1)}, bf16[16,4,2,128,128]{4,3,2,1,0:T(8,128)(2,1)S(1)}, u32[]{:S(2)}) copy-start(bf16[16,4,2,128,128]{4,3,2,1,0:T(8,128)(2,1)S(1)} %gather_pages.3.pages_in) | copy-start | bytes 12582916
  132.2 14.6 %copy-start.6 = (bf16[1,1024,512]{2,1,0:T(8,128)(2,1)S(1)}, bf16[1,1024,512]{2,1,0:T(8,128)(2,1)}, u32[]{:S(2)}) copy-start(bf16[1,1024,512]{2,1,0:T(8,128)(2,1)} %param.15) | copy-start | bytes 3145732
  132.2 45.5 %copy-start.9 = (s32[640]{0:T(1024)S(1)}, s32[640]{0:T(1024)}, u32[]{:S(2)}) copy-start(s32[640]{0:T(1024)} %copy-done.8) | copy-start | bytes 7684
  142.2 58.3 %all-to-all-start.3 = ((bf16[16,4,2,128,128]{4,3,2,1,0:T(8,128)(2,1)}), bf16[16,4,2,128,128]{4,3,2,1,0:T(8,128)(2,1)}, u32[]{:S(2)}, u32[]{:S(2)}) async-start(bf16[16,4,2,128,128]{4,3,2,1,0:T(8,128)(2,1)} %write_tokens.1), calls=%async_computation.3 | async-start | bytes 8388608 | tf_op jit(solution)/shard_map/all_to_all | solution.py:463
  149.1 6.8 %collective-permute-start = (f32[64,512]{1,0:T(8,128)S(1)}, f32[64,512]{1,0:T(8,128)S(1)}, u32[]{:S(2)}, u32[]{:S(2)}) collective-permute-start(f32[64,512]{1,0:T(8,128)S(1)} %get-tuple-element.19), channel_id=1, source_target_pairs={{0,1},{1,0},{2,3},{3,2},{4,5},{5,4},{6,7},{7,6},{8,9},{9,8},{10,11... | collective-permute-start | bytes 393224 | tf_op jit(solution)/shard_map/ppermute | solution.py:43
  149.1 8.4 %collective-permute-start.1 = (f32[64,512]{1,0:T(8,128)S(1)}, f32[64,512]{1,0:T(8,128)S(1)}, u32[]{:S(2)}, u32[]{:S(2)}) collective-permute-start(f32[64,512]{1,0:T(8,128)S(1)} %get-tuple-element.20), channel_id=1, source_target_pairs={{0,2},{1,3},{2,4},{3,5},{4,6},{5,7},{6,0},{7,1},{8,10},{9,11},{10,... | collective-permute-start | bytes 393224 | tf_op jit(solution)/shard_map/ppermute | solution.py:43
  151.0 8.9 %collective-permute-start.2 = (f32[64,512]{1,0:T(8,128)S(1)}, f32[64,512]{1,0:T(8,128)S(1)}, u32[]{:S(2)}, u32[]{:S(2)}) collective-permute-start(f32[64,512]{1,0:T(8,128)S(1)} %get-tuple-element.21), channel_id=1, source_target_pairs={{0,3},{1,2},{2,5},{3,4},{4,7},{5,6},{6,1},{7,0},{8,11},{9,10},{10,... | collective-permute-start | bytes 393224 | tf_op jit(solution)/shard_map/ppermute | solution.py:43
  152.8 11.7 %collective-permute-start.3 = (f32[64,512]{1,0:T(8,128)S(1)}, f32[64,512]{1,0:T(8,128)S(1)}, u32[]{:S(2)}, u32[]{:S(2)}) collective-permute-start(f32[64,512]{1,0:T(8,128)S(1)} %get-tuple-element.22), channel_id=1, source_target_pairs={{0,4},{1,5},{2,6},{3,7},{4,0},{5,1},{6,2},{7,3},{8,12},{9,13},{10,... | collective-permute-start | bytes 393224 | tf_op jit(solution)/shard_map/ppermute | solution.py:43
  154.7 11.8 %collective-permute-start.4 = (f32[64,512]{1,0:T(8,128)S(1)}, f32[64,512]{1,0:T(8,128)S(1)}, u32[]{:S(2)}, u32[]{:S(2)}) collective-permute-start(f32[64,512]{1,0:T(8,128)S(1)} %get-tuple-element.23), channel_id=1, source_target_pairs={{0,5},{1,4},{2,7},{3,6},{4,1},{5,0},{6,3},{7,2},{8,13},{9,12},{10,... | collective-permute-start | bytes 393224 | tf_op jit(solution)/shard_map/ppermute | solution.py:43
  155.9 11.2 %copy-start.12 = (f32[64,512]{1,0:T(8,128)}, f32[64,512]{1,0:T(8,128)S(1)}, u32[]{:S(2)}) copy-start(f32[64,512]{1,0:T(8,128)S(1)} %collective-permute-done.refs_1_) | copy-start | bytes 393220
  155.9 10.6 %collective-permute-start.5 = (f32[64,512]{1,0:T(8,128)S(1)}, f32[64,512]{1,0:T(8,128)S(1)}, u32[]{:S(2)}, u32[]{:S(2)}) collective-permute-start(f32[64,512]{1,0:T(8,128)S(1)} %get-tuple-element.24), channel_id=1, source_target_pairs={{0,6},{1,7},{2,0},{3,1},{4,2},{5,3},{6,4},{7,5},{8,14},{9,15},{10,... | collective-permute-start | bytes 393224 | tf_op jit(solution)/shard_map/ppermute | solution.py:43
  157.5 9.7 %copy-start.13 = (f32[64,512]{1,0:T(8,128)}, f32[64,512]{1,0:T(8,128)S(1)}, u32[]{:S(2)}) copy-start(f32[64,512]{1,0:T(8,128)S(1)} %collective-permute-done.1.refs_2_) | copy-start | bytes 393220
  157.5 9.7 %collective-permute-start.6 = (f32[64,512]{1,0:T(8,128)S(1)}, f32[64,512]{1,0:T(8,128)S(1)}, u32[]{:S(2)}, u32[]{:S(2)}) collective-permute-start(f32[64,512]{1,0:T(8,128)S(1)} %get-tuple-element.25), channel_id=1, source_target_pairs={{0,7},{1,6},{2,1},{3,0},{4,3},{5,2},{6,5},{7,4},{8,15},{9,14},{10,... | collective-permute-start | bytes 393224 | tf_op jit(solution)/shard_map/ppermute | solution.py:43
  159.9 7.3 %copy-start.14 = (f32[64,512]{1,0:T(8,128)}, f32[64,512]{1,0:T(8,128)S(1)}, u32[]{:S(2)}) copy-start(f32[64,512]{1,0:T(8,128)S(1)} %collective-permute-done.2.refs_3_) | copy-start | bytes 393220
  164.5 2.7 %copy-start.15 = (f32[64,512]{1,0:T(8,128)}, f32[64,512]{1,0:T(8,128)S(1)}, u32[]{:S(2)}) copy-start(f32[64,512]{1,0:T(8,128)S(1)} %collective-permute-done.3.refs_4_) | copy-start | bytes 393220
  169.8 7.6 %collective-permute-start.13 = (bf16[64,512]{1,0:T(8,128)(2,1)}, bf16[64,512]{1,0:T(8,128)(2,1)S(1)}, u32[]{:S(2)}, u32[]{:S(2)}) collective-permute-start(bf16[64,512]{1,0:T(8,128)(2,1)} %total_rows.1.refs_0_), channel_id=1, source_target_pairs={{0,7},{1,6},{2,1},{3,0},{4,3},{5,2},{6,5},{7,4},{8,15},{9,14},{10,... | collective-permute-start | bytes 196616 | tf_op jit(solution)/shard_map/ppermute | solution.py:43
  172.4 5.2 %collective-permute-start.12 = (bf16[64,512]{1,0:T(8,128)(2,1)}, bf16[64,512]{1,0:T(8,128)(2,1)S(1)}, u32[]{:S(2)}, u32[]{:S(2)}) collective-permute-start(bf16[64,512]{1,0:T(8,128)(2,1)} %total_rows.1.refs_0_), channel_id=1, source_target_pairs={{0,6},{1,7},{2,0},{3,1},{4,2},{5,3},{6,4},{7,5},{8,14},{9,15},{10,... | collective-permute-start | bytes 196616 | tf_op jit(solution)/shard_map/ppermute | solution.py:43
  173.6 9.7 %collective-permute-start.11 = (bf16[64,512]{1,0:T(8,128)(2,1)}, bf16[64,512]{1,0:T(8,128)(2,1)S(1)}, u32[]{:S(2)}, u32[]{:S(2)}) collective-permute-start(bf16[64,512]{1,0:T(8,128)(2,1)} %total_rows.1.refs_0_), channel_id=1, source_target_pairs={{0,5},{1,4},{2,7},{3,6},{4,1},{5,0},{6,3},{7,2},{8,13},{9,12},{10,... | collective-permute-start | bytes 196616 | tf_op jit(solution)/shard_map/ppermute | solution.py:43
  174.3 9.1 %collective-permute-start.10 = (bf16[64,512]{1,0:T(8,128)(2,1)}, bf16[64,512]{1,0:T(8,128)(2,1)S(1)}, u32[]{:S(2)}, u32[]{:S(2)}) collective-permute-start(bf16[64,512]{1,0:T(8,128)(2,1)} %total_rows.1.refs_0_), channel_id=1, source_target_pairs={{0,4},{1,5},{2,6},{3,7},{4,0},{5,1},{6,2},{7,3},{8,12},{9,13},{10,... | collective-permute-start | bytes 196616 | tf_op jit(solution)/shard_map/ppermute | solution.py:43
  176.1 7.3 %collective-permute-start.9 = (bf16[64,512]{1,0:T(8,128)(2,1)}, bf16[64,512]{1,0:T(8,128)(2,1)S(1)}, u32[]{:S(2)}, u32[]{:S(2)}) collective-permute-start(bf16[64,512]{1,0:T(8,128)(2,1)} %total_rows.1.refs_0_), channel_id=1, source_target_pairs={{0,3},{1,2},{2,5},{3,4},{4,7},{5,6},{6,1},{7,0},{8,11},{9,10},{10,... | collective-permute-start | bytes 196616 | tf_op jit(solution)/shard_map/ppermute | solution.py:43
  177.4 6.0 %copy-start.19 = (bf16[64,512]{1,0:T(8,128)(2,1)}, bf16[64,512]{1,0:T(8,128)(2,1)S(1)}, u32[]{:S(2)}) copy-start(bf16[64,512]{1,0:T(8,128)(2,1)S(1)} %collective-permute-done.13.refs_7_) | copy-start | bytes 196612
  177.4 6.3 %collective-permute-start.8 = (bf16[64,512]{1,0:T(8,128)(2,1)}, bf16[64,512]{1,0:T(8,128)(2,1)S(1)}, u32[]{:S(2)}, u32[]{:S(2)}) collective-permute-start(bf16[64,512]{1,0:T(8,128)(2,1)} %total_rows.1.refs_0_), channel_id=1, source_target_pairs={{0,2},{1,3},{2,4},{3,5},{4,6},{5,7},{6,0},{7,1},{8,10},{9,11},{10,... | collective-permute-start | bytes 196616 | tf_op jit(solution)/shard_map/ppermute | solution.py:43
  177.6 5.8 %copy-start.20 = (bf16[64,512]{1,0:T(8,128)(2,1)}, bf16[64,512]{1,0:T(8,128)(2,1)S(1)}, u32[]{:S(2)}) copy-start(bf16[64,512]{1,0:T(8,128)(2,1)S(1)} %collective-permute-done.12.refs_6_) | copy-start | bytes 196612
  177.6 6.1 %collective-permute-start.7 = (bf16[64,512]{1,0:T(8,128)(2,1)}, bf16[64,512]{1,0:T(8,128)(2,1)S(1)}, u32[]{:S(2)}, u32[]{:S(2)}) collective-permute-start(bf16[64,512]{1,0:T(8,128)(2,1)} %total_rows.1.refs_0_), channel_id=1, source_target_pairs={{0,1},{1,0},{2,3},{3,2},{4,5},{5,4},{6,7},{7,6},{8,9},{9,8},{10,11... | collective-permute-start | bytes 196616 | tf_op jit(solution)/shard_map/ppermute | solution.py:43
  (15 other events, 13.4 us)

commit v3 on v2

--- a/solution.py
+++ b/solution.py
@@ -36,6 +36,18 @@
 
 def cost(flops, moved):
     return pl.CostEstimate(flops=flops, bytes_accessed=moved, transcendentals=0)
+
+
+def move(array, dy, dx):
+    pairs = [(y * SIDE + x, ((y + dy) % SIDE) * SIDE + (x + dx) % SIDE) for y in range(SIDE) for x in range(SIDE)]
+    return lax.ppermute(array, "grp", pairs)
+
+
+def steps_back(array, dy, dx):
+    line = [array]
+    for _ in range(SIDE - 1):
+        line.append(move(line[-1], -dy, -dx))
+    return line
 
 
 def move_part(array, dz, dc):
@@ -140,7 +152,7 @@
     step = pl.program_id(0)
     block = SLOTS // pl.num_programs(0)
     scale = 1.0 / math.sqrt(HD)
-    heads = out_ref.shape[2] // HD - 2
+    heads = out_ref.shape[1] // HD - 2
     blocks = heads + 2
     qr = STEPS * heads
 
@@ -205,9 +217,7 @@
     def _():
         for c in range(blocks):
             source = done if c < heads else proj
-            part = source[c * ROWS:(c + 1) * ROWS, :].astype(out_ref.dtype)
-            for g in range(out_ref.shape[0]):
-                out_ref[g, :, c * HD:(c + 1) * HD] = part
+            out_ref[:, c * HD:(c + 1) * HD] = source[c * ROWS:(c + 1) * ROWS, :].astype(out_ref.dtype)
         for kv in range(2):
             new_ref[kv] = proj[(heads + kv) * ROWS:(heads + kv + 1) * ROWS, :]
 
@@ -215,7 +225,7 @@
 def attend(ints, sums, pool):
     blocks = sums.shape[1] // ROWS
     whole = lambda a: pl.BlockSpec(a.shape, lambda i, *_: (0,) * len(a.shape))
-    out = jax.ShapeDtypeStruct((sums.shape[0], ROWS, blocks * HD), jnp.bfloat16)
+    out = jax.ShapeDtypeStruct((ROWS, blocks * HD), jnp.bfloat16)
     new = jax.ShapeDtypeStruct((2, ROWS, HD), jnp.float32)
     return pl.pallas_call(
         attend_kernel,
@@ -231,6 +241,32 @@
         cost_estimate=cost(4 * SLOTS * MAXP * PAGE * HD * 16, 10 * 2**20),
         name="attend",
     )(ints, sums, pool)
+
+
+def arrange_kernel(*refs):
+    ins, out = refs[:-1], refs[-1]
+    me = lax.axis_index("grp")
+    y, x = me // SIDE, me % SIDE
+    pieces = len(ins) // SIDE
+    for i, piece in enumerate(ins):
+        part, ix = divmod(i, SIDE)
+        each = SIDE // pieces
+        for k in range(each):
+            iy = part * each + k
+            out[((y + iy) % SIDE) * SIDE + (x + ix) % SIDE] = piece[k]
+
+
+def arrange(arrays):
+    shape = (SIDE * SIDE,) + arrays[0].shape[1:]
+    return pl.pallas_call(
+        arrange_kernel,
+        out_shape=jax.ShapeDtypeStruct(shape, arrays[0].dtype),
+        in_specs=[VMEM] * len(arrays),
+        out_specs=VMEM,
+        compiler_params=params(20),
+        cost_estimate=cost(0, 3 * 2**20),
+        name="arrange",
+    )(*arrays)
 
 
 def output_kernel(rows_ref, w_ref, *refs):
@@ -475,8 +511,10 @@
     near = exchange(lax.optimization_barrier((near, sums))[0])
     mine, new = attend(ints, sums, kv_pool)
     far = write_tokens(CUTS[1], ints, new, far)
-    rows = exchange(lax.optimization_barrier((mine, near))[0])
-    far = exchange(lax.optimization_barrier((far, rows))[0])
+    line = steps_back(mine, 1, 0)
+    pieces = steps_back(jnp.stack(line[:2]), 0, 1) + steps_back(jnp.stack(line[2:]), 0, 1)
+    far = exchange(lax.optimization_barrier((far, pieces))[0])
+    rows = arrange(pieces)
 
     parts = output_rows(rows, w_out.reshape(heads * HD, width))
     distances = [divmod(i, CORES) for i in range(SIDE * CORES)]

time: 205 us -> 204 us (level)
  waiting for transfers between devices: 119 us -> 112 us
  starting transfers between devices: 37.7 us -> 43.4 us
    all_to_all x4 -> x3, waiting for transfers between devices: 110 us -> 39.4 us  [exchange(): return lax.all_to_all(array, 'grp', split_axis=0, concat_axis=0, tiled=True)]
    ppermute x0 -> x9, waiting for transfers between devices: none -> 57.6 us  [move(): return lax.ppermute(array, 'grp', pairs)]
    ppermute x0 -> x9, starting transfers between devices: none -> 10.1 us  [move(): return lax.ppermute(array, 'grp', pairs)]
    ppermute x14, waiting for transfers between devices: 9.18 us -> 14.9 us  [move_part(): return lax.ppermute(array, 'tp', pairs)]
    all_to_all x4 -> x3, starting transfers between devices: 20.7 us -> 16.2 us  [exchange(): return lax.all_to_all(array, 'grp', split_axis=0, concat_axis=0, tiled=True)]
    unnamed x58 -> x60, local copies, waits for them, and re-layouts: 15.5 us -> 16 us
  transfers between devices with their start and end apart: 18 -> 26, of which waited for: 10 -> 18; matrix products, arithmetic and copies ran while one was open for 0% -> 0% of each run, Pallas kernels for 13% -> 13%
where the time goes in v3:
time: 204 us; the launch traced here: 203 us
  waiting for transfers between devices  112 us (55%)
  starting transfers between devices  43.4 us (21%)
  Pallas kernels  30.2 us (15%)
  local copies, waits for them, and re-layouts  16.8 us (8%)
    ppermute x9, waiting for transfers between devices, move(): return lax.ppermute(array, 'grp', pairs)  57.6 us
    all_to_all x3, waiting for transfers between devices, exchange(): return lax.all_to_all(array, 'grp', split_axis=0, concat_axis=0, tiled=True)  39.4 us
    ppermute x14, starting transfers between devices, move_part(): return lax.ppermute(array, 'tp', pairs)  17 us
    all_to_all x3, starting transfers between devices, exchange(): return lax.all_to_all(array, 'grp', split_axis=0, concat_axis=0, tiled=True)  16.2 us
    unnamed x60, local copies, waits for them, and re-layouts  16 us
    ppermute x14, waiting for transfers between devices, move_part(): return lax.ppermute(array, 'tp', pairs)  14.9 us
    ppermute x9, starting transfers between devices, move(): return lax.ppermute(array, 'grp', pairs)  10.1 us
    pallas_call x2, Pallas kernels, gather_pages(): pl.pallas_call(functools.partial(gather_kernel, low), out_shape=shape, in...  6.25 us
  transfers between devices with their start and end apart: 26, of which 18 were waited for; matrix products, arithmetic and copies ran while one was open for 0% of the time, Pallas kernels for 13%

profile of v3, /device:TPU:0, one launch (start us, length us, event | category | flops | bytes accessed | tf_op | source)
XLA Modules:
  0.0 203.2 jit_solution(15751115733048410145)
XLA Ops:
  6.1 7.1 %all-to-all-start = ((f32[16,328,128]{2,1,0:T(8,128)}), f32[16,328,128]{2,1,0:T(8,128)S(1)}, u32[]{:S(2)}, u32[]{:S(2)}) async-start(f32[16,328,128]{2,1,0:T(8,128)} %copy-done.3), calls=%async_computation | async-start | bytes 5373952 | tf_op jit(solution)/shard_map/all_to_all | solution.py:499
  13.3 3.2 %gather_pages.3 = bf16[16,4,2,128,128]{4,3,2,1,0:T(8,128)(2,1)S(1)} custom-call(s32[640]{0:T(1024)S(1)} %pad_add_fusion.ints_ref, bf16[128,2,1,128,128]{4,3,2,1,0:T(8,128)(2,1)} %pool_ref.3), custom_call_target="tpu_custom_call" | custom-call | bytes 8388608 | tf_op jit(solution)/shard_map/gather_pages/pallas_call | solution.py:137
  16.5 2.0 copy-done.2
  18.5 35.4 %all-to-all-done.refs_0_ = f32[16,328,128]{2,1,0:T(8,128)S(1)} async-done(((f32[16,328,128]{2,1,0:T(8,128)}), f32[16,328,128]{2,1,0:T(8,128)S(1)}, u32[]{:S(2)}, u32[]{:S(2)}) %all-to-all-start) | async-done | bytes 2687008 | tf_op jit(solution)/shard_map/all_to_all | solution.py:499
  53.9 4.6 %all-to-all-start.2 = ((bf16[16,4,2,128,128]{4,3,2,1,0:T(8,128)(2,1)}), bf16[16,4,2,128,128]{4,3,2,1,0:T(8,128)(2,1)}, u32[]{:S(2)}, u32[]{:S(2)}) async-start(bf16[16,4,2,128,128]{4,3,2,1,0:T(8,128)(2,1)} %copy-done.2), calls=%async_computation.2 | async-start | bytes 8388608 | tf_op jit(solution)/shard_map/all_to_all | solution.py:499
  58.5 3.4 %copy-done = bf16[128,2,1,128,128]{4,3,2,1,0:T(8,128)(2,1)S(1)} copy-done((bf16[128,2,1,128,128]{4,3,2,1,0:T(8,128)(2,1)S(1)}, bf16[128,2,1,128,128]{4,3,2,1,0:T(8,128)(2,1)}, u32[]{:S(2)}) %copy-start) | copy-done | bytes 8388632
  61.8 4.7 %attend.1 = (bf16[32,1280]{1,0:T(8,128)(2,1)S(1)}, f32[2,32,128]{2,1,0:T(8,128)S(1)}) custom-call(s32[640]{0:T(1024)S(1)} %pad_add_fusion.ints_ref, f32[16,328,128]{2,1,0:T(8,128)S(1)} %all-to-all-done.refs_0_, bf16[128,2,1,128,128]{4,3,2,1,0:T(8,128)(2,1)S(1)} %copy-done), custom_call_target="tpu_custom_call" | custom-call | flops 134217728 | bytes 10485760 | tf_op jit(solution)/shard_map/attend/pallas_call | solution.py:230
  67.2 3.0 %collective-permute-start = (bf16[32,1280]{1,0:T(8,128)(2,1)S(1)}, bf16[32,1280]{1,0:T(8,128)(2,1)S(1)}, u32[]{:S(2)}, u32[]{:S(2)}) collective-permute-start(bf16[32,1280]{1,0:T(8,128)(2,1)S(1)} %get-tuple-element.14), channel_id=1, source_target_pairs={{0,96},{8,104},{16,112},{24,120},{32,0},{40,8},{48,16},{56,24},{64... | collective-permute-start | bytes 245768 | tf_op jit(solution)/shard_map/ppermute | solution.py:43
  70.2 36.8 %collective-permute-done = bf16[32,1280]{1,0:T(8,128)(2,1)S(1)} collective-permute-done((bf16[32,1280]{1,0:T(8,128)(2,1)S(1)}, bf16[32,1280]{1,0:T(8,128)(2,1)S(1)}, u32[]{:S(2)}, u32[]{:S(2)}) %collective-permute-start) | collective-permute-done | bytes 81952 | tf_op jit(solution)/shard_map/ppermute | solution.py:43
  107.0 4.8 %collective-permute-done.4 = bf16[32,1280]{1,0:T(8,128)(2,1)S(1)} collective-permute-done((bf16[32,1280]{1,0:T(8,128)(2,1)S(1)}, bf16[32,1280]{1,0:T(8,128)(2,1)S(1)}, u32[]{:S(2)}, u32[]{:S(2)}) %collective-permute-start.4) | collective-permute-done | bytes 81952 | tf_op jit(solution)/shard_map/ppermute | solution.py:43
  114.4 1.9 collective-permute-done.5
  117.1 5.7 %collective-permute-done.1.refs_1_ = bf16[2,32,1280]{2,1,0:T(8,128)(2,1)S(1)} collective-permute-done((bf16[2,32,1280]{2,1,0:T(8,128)(2,1)S(1)}, bf16[2,32,1280]{2,1,0:T(8,128)(2,1)S(1)}, u32[]{:S(2)}, u32[]{:S(2)}) %collective-permute-start.1) | collective-permute-done | bytes 163872 | tf_op jit(solution)/shard_map/ppermute | solution.py:43
  123.8 2.5 %collective-permute-done.6.refs_5_ = bf16[2,32,1280]{2,1,0:T(8,128)(2,1)S(1)} collective-permute-done((bf16[2,32,1280]{2,1,0:T(8,128)(2,1)S(1)}, bf16[2,32,1280]{2,1,0:T(8,128)(2,1)S(1)}, u32[]{:S(2)}, u32[]{:S(2)}) %collective-permute-start.6) | collective-permute-done | bytes 163872 | tf_op jit(solution)/shard_map/ppermute | solution.py:43
  127.2 2.8 %collective-permute-done.2.refs_2_ = bf16[2,32,1280]{2,1,0:T(8,128)(2,1)S(1)} collective-permute-done((bf16[2,32,1280]{2,1,0:T(8,128)(2,1)S(1)}, bf16[2,32,1280]{2,1,0:T(8,128)(2,1)S(1)}, u32[]{:S(2)}, u32[]{:S(2)}) %collective-permute-start.2) | collective-permute-done | bytes 163872 | tf_op jit(solution)/shard_map/ppermute | solution.py:43
  130.6 2.9 %collective-permute-done.7.refs_6_ = bf16[2,32,1280]{2,1,0:T(8,128)(2,1)S(1)} collective-permute-done((bf16[2,32,1280]{2,1,0:T(8,128)(2,1)S(1)}, bf16[2,32,1280]{2,1,0:T(8,128)(2,1)S(1)}, u32[]{:S(2)}, u32[]{:S(2)}) %collective-permute-start.7) | collective-permute-done | bytes 163872 | tf_op jit(solution)/shard_map/ppermute | solution.py:43
  134.9 3.0 %gather_pages.2.pages_in = bf16[16,4,2,128,128]{4,3,2,1,0:T(8,128)(2,1)S(1)} custom-call(s32[640]{0:T(1024)S(1)} %pad_add_fusion.ints_ref, bf16[128,2,1,128,128]{4,3,2,1,0:T(8,128)(2,1)} %pool_ref.3), custom_call_target="tpu_custom_call" | custom-call | bytes 8388608 | tf_op jit(solution)/shard_map/gather_pages/pallas_call | solution.py:137
  138.0 2.1 %copy-done.1 = bf16[16,4,2,128,128]{4,3,2,1,0:T(8,128)(2,1)} copy-done((bf16[16,4,2,128,128]{4,3,2,1,0:T(8,128)(2,1)}, bf16[16,4,2,128,128]{4,3,2,1,0:T(8,128)(2,1)S(1)}, u32[]{:S(2)}) %copy-start.1) | copy-done | bytes 4194328
  140.0 3.4 %write_tokens.1 = bf16[16,4,2,128,128]{4,3,2,1,0:T(8,128)(2,1)} custom-call(s32[640]{0:T(1024)} %copy-done.9, f32[2,32,128]{2,1,0:T(8,128)} %copy-done.12, bf16[16,4,2,128,128]{4,3,2,1,0:T(8,128)(2,1)} %copy-done.1), custom_call_target="tpu_custom_call", output_to_operand_aliasing={{}: (2, {})} | custom-call | bytes 1048576 | tf_op jit(solution)/shard_map/write_tokens/pallas_call | solution.py:458
  144.1 4.5 %all-to-all-start.1 = ((bf16[16,4,2,128,128]{4,3,2,1,0:T(8,128)(2,1)}), bf16[16,4,2,128,128]{4,3,2,1,0:T(8,128)(2,1)}, u32[]{:S(2)}, u32[]{:S(2)}) async-start(bf16[16,4,2,128,128]{4,3,2,1,0:T(8,128)(2,1)} %write_tokens.1), calls=%async_computation.1 | async-start | bytes 8388608 | tf_op jit(solution)/shard_map/all_to_all | solution.py:499
  152.0 1.9 collective-permute-start.10
  153.9 1.8 collective-permute-start.11
  155.7 2.0 collective-permute-start.12
  162.9 4.6 %collective-permute-done.12.refs_4_ = f32[64,512]{1,0:T(8,128)S(1)} collective-permute-done((f32[64,512]{1,0:T(8,128)S(1)}, f32[64,512]{1,0:T(8,128)S(1)}, u32[]{:S(2)}, u32[]{:S(2)}) %collective-permute-start.12) | collective-permute-done | bytes 131104 | tf_op jit(solution)/shard_map/ppermute | solution.py:55
  167.4 2.0 %collective-permute-done.13.refs_5_ = f32[64,512]{1,0:T(8,128)S(1)} collective-permute-done((f32[64,512]{1,0:T(8,128)S(1)}, f32[64,512]{1,0:T(8,128)S(1)}, u32[]{:S(2)}, u32[]{:S(2)}) %collective-permute-start.13) | collective-permute-done | bytes 131104 | tf_op jit(solution)/shard_map/ppermute | solution.py:55
  170.8 2.0 total_rows.1.refs_0_
  172.7 2.6 %collective-permute-start.22 = (bf16[64,512]{1,0:T(8,128)(2,1)}, bf16[64,512]{1,0:T(8,128)(2,1)S(1)}, u32[]{:S(2)}, u32[]{:S(2)}) collective-permute-start(bf16[64,512]{1,0:T(8,128)(2,1)} %total_rows.1.refs_0_), channel_id=1, source_target_pairs={{0,7},{1,6},{2,1},{3,0},{4,3},{5,2},{6,5},{7,4},{8,15},{9,14},{10,... | collective-permute-start | bytes 196616 | tf_op jit(solution)/shard_map/ppermute | solution.py:55
  177.3 1.8 collective-permute-start.19
  184.4 2.3 %collective-permute-done.17.refs_2_ = bf16[64,512]{1,0:T(8,128)(2,1)S(1)} collective-permute-done((bf16[64,512]{1,0:T(8,128)(2,1)}, bf16[64,512]{1,0:T(8,128)(2,1)S(1)}, u32[]{:S(2)}, u32[]{:S(2)}) %collective-permute-start.17) | collective-permute-done | bytes 65568 | tf_op jit(solution)/shard_map/ppermute | solution.py:55
  187.9 1.9 order_rows.1
  189.8 5.5 %insert_tokens.1.cache_in = bf16[16,8,2,1,128,128]{5,4,3,2,1,0:T(8,128)(2,1)} custom-call(s32[640]{0:T(1024)S(1)} %copy-done.10, bf16[16,32,1280]{2,1,0:T(8,128)(2,1)S(1)} %arrange.1.rows_ref, bf16[16,4,2,128,128]{4,3,2,1,0:T(8,128)(2,1)} %all-to-all-done.2.pages_ref), custom_call_target="tpu_custom_call" | custom-call | bytes 8388608 | tf_op jit(solution)/shard_map/insert_tokens/pallas_call | solution.py:389
  195.3 4.0 %all-to-all-done.1.pages_ref = bf16[16,4,2,128,128]{4,3,2,1,0:T(8,128)(2,1)} async-done(((bf16[16,4,2,128,128]{4,3,2,1,0:T(8,128)(2,1)}), bf16[16,4,2,128,128]{4,3,2,1,0:T(8,128)(2,1)}, u32[]{:S(2)}, u32[]{:S(2)}) %all-to-all-start.1) | async-done | bytes 4194336 | tf_op jit(solution)/shard_map/all_to_all | solution.py:499
  199.4 3.8 %settle.1 = bf16[16,8,2,1,128,128]{5,4,3,2,1,0:T(8,128)(2,1)} custom-call(bf16[16,4,2,128,128]{4,3,2,1,0:T(8,128)(2,1)} %all-to-all-done.1.pages_ref, bf16[16,8,2,1,128,128]{5,4,3,2,1,0:T(8,128)(2,1)} %insert_tokens.1.cache_in), custom_call_target="tpu_custom_call", output_to_operand_aliasing={{}: (1, {})} | custom-call | bytes 8388608 | tf_op jit(solution)/shard_map/settle/pallas_call | solution.py:485
  (96 shorter events, 32.1 us)
Async XLA Ops:
  3.7 9.6 %copy-start.28 = (s32[256]{0:T(256)S(1)}, s32[256]{0:T(256)}, u32[]{:S(2)}) copy-start(s32[256]{0:T(256)} %param.8) | copy-start | bytes 3076
  3.7 9.6 %copy-start.29 = (s32[1,128]{1,0:T(1,128)S(1)}, s32[1,128]{1,0:T(1,128)}, u32[]{:S(2)}) copy-start(s32[1,128]{1,0:T(1,128)} %param.10) | copy-start | bytes 1540
  6.1 47.8 %all-to-all-start = ((f32[16,328,128]{2,1,0:T(8,128)}), f32[16,328,128]{2,1,0:T(8,128)S(1)}, u32[]{:S(2)}, u32[]{:S(2)}) async-start(f32[16,328,128]{2,1,0:T(8,128)} %copy-done.3), calls=%async_computation | async-start | bytes 5373952 | tf_op jit(solution)/shard_map/all_to_all | solution.py:499
  13.3 121.6 %copy-start.9 = (s32[640]{0:T(1024)}, s32[640]{0:T(1024)S(1)}, u32[]{:S(2)}) copy-start(s32[640]{0:T(1024)S(1)} %pad_add_fusion.ints_ref) | copy-start | bytes 7684
  53.9 90.3 %all-to-all-start.2 = ((bf16[16,4,2,128,128]{4,3,2,1,0:T(8,128)(2,1)}), bf16[16,4,2,128,128]{4,3,2,1,0:T(8,128)(2,1)}, u32[]{:S(2)}, u32[]{:S(2)}) async-start(bf16[16,4,2,128,128]{4,3,2,1,0:T(8,128)(2,1)} %copy-done.2), calls=%async_computation.2 | async-start | bytes 8388608 | tf_op jit(solution)/shard_map/all_to_all | solution.py:499
  67.2 39.9 %collective-permute-start = (bf16[32,1280]{1,0:T(8,128)(2,1)S(1)}, bf16[32,1280]{1,0:T(8,128)(2,1)S(1)}, u32[]{:S(2)}, u32[]{:S(2)}) collective-permute-start(bf16[32,1280]{1,0:T(8,128)(2,1)S(1)} %get-tuple-element.14), channel_id=1, source_target_pairs={{0,96},{8,104},{16,112},{24,120},{32,0},{40,8},{48,16},{56,24},{64... | collective-permute-start | bytes 245768 | tf_op jit(solution)/shard_map/ppermute | solution.py:43
  107.0 4.8 %collective-permute-start.4 = (bf16[32,1280]{1,0:T(8,128)(2,1)S(1)}, bf16[32,1280]{1,0:T(8,128)(2,1)S(1)}, u32[]{:S(2)}, u32[]{:S(2)}) collective-permute-start(bf16[32,1280]{1,0:T(8,128)(2,1)S(1)} %collective-permute-done), channel_id=1, source_target_pairs={{0,96},{8,104},{16,112},{24,120},{32,0},{40,8},{48,16},{56,24},{64... | collective-permute-start | bytes 245768 | tf_op jit(solution)/shard_map/ppermute | solution.py:43
  111.9 4.4 %collective-permute-start.5 = (bf16[32,1280]{1,0:T(8,128)(2,1)S(1)}, bf16[32,1280]{1,0:T(8,128)(2,1)S(1)}, u32[]{:S(2)}, u32[]{:S(2)}) collective-permute-start(bf16[32,1280]{1,0:T(8,128)(2,1)S(1)} %collective-permute-done.4), channel_id=1, source_target_pairs={{0,96},{8,104},{16,112},{24,120},{32,0},{40,8},{48,16},{56,24},{64... | collective-permute-start | bytes 245768 | tf_op jit(solution)/shard_map/ppermute | solution.py:43
  113.5 9.3 %collective-permute-start.1 = (bf16[2,32,1280]{2,1,0:T(8,128)(2,1)S(1)}, bf16[2,32,1280]{2,1,0:T(8,128)(2,1)S(1)}, u32[]{:S(2)}, u32[]{:S(2)}) collective-permute-start(bf16[2,32,1280]{2,1,0:T(8,128)(2,1)S(1)} %pad_maximum_fusion.refs_0_), channel_id=1, source_target_pairs={{0,24},{8,0},{16,8},{24,16},{32,56},{40,32},{48,40},{56,48},{64,88... | collective-permute-start | bytes 491528 | tf_op jit(solution)/shard_map/ppermute | solution.py:43
  116.3 10.1 %collective-permute-start.6 = (bf16[2,32,1280]{2,1,0:T(8,128)(2,1)S(1)}, bf16[2,32,1280]{2,1,0:T(8,128)(2,1)S(1)}, u32[]{:S(2)}, u32[]{:S(2)}) collective-permute-start(bf16[2,32,1280]{2,1,0:T(8,128)(2,1)S(1)} %pad_maximum_fusion.1.refs_4_), channel_id=1, source_target_pairs={{0,24},{8,0},{16,8},{24,16},{32,56},{40,32},{48,40},{56,48},{64,88... | collective-permute-start | bytes 491528 | tf_op jit(solution)/shard_map/ppermute | solution.py:43
  122.9 7.1 %collective-permute-start.2 = (bf16[2,32,1280]{2,1,0:T(8,128)(2,1)S(1)}, bf16[2,32,1280]{2,1,0:T(8,128)(2,1)S(1)}, u32[]{:S(2)}, u32[]{:S(2)}) collective-permute-start(bf16[2,32,1280]{2,1,0:T(8,128)(2,1)S(1)} %collective-permute-done.1.refs_1_), channel_id=1, source_target_pairs={{0,24},{8,0},{16,8},{24,16},{32,56},{40,32},{48,40},{56,48},{64,88... | collective-permute-start | bytes 491528 | tf_op jit(solution)/shard_map/ppermute | solution.py:43
  126.4 7.1 %collective-permute-start.7 = (bf16[2,32,1280]{2,1,0:T(8,128)(2,1)S(1)}, bf16[2,32,1280]{2,1,0:T(8,128)(2,1)S(1)}, u32[]{:S(2)}, u32[]{:S(2)}) collective-permute-start(bf16[2,32,1280]{2,1,0:T(8,128)(2,1)S(1)} %collective-permute-done.6.refs_5_), channel_id=1, source_target_pairs={{0,24},{8,0},{16,8},{24,16},{32,56},{40,32},{48,40},{56,48},{64,88... | collective-permute-start | bytes 491528 | tf_op jit(solution)/shard_map/ppermute | solution.py:43
  130.0 13.4 %collective-permute-start.3 = (bf16[2,32,1280]{2,1,0:T(8,128)(2,1)S(1)}, bf16[2,32,1280]{2,1,0:T(8,128)(2,1)S(1)}, u32[]{:S(2)}, u32[]{:S(2)}) collective-permute-start(bf16[2,32,1280]{2,1,0:T(8,128)(2,1)S(1)} %collective-permute-done.2.refs_2_), channel_id=1, source_target_pairs={{0,24},{8,0},{16,8},{24,16},{32,56},{40,32},{48,40},{56,48},{64,88... | collective-permute-start | bytes 491528 | tf_op jit(solution)/shard_map/ppermute | solution.py:43
  133.5 9.9 %collective-permute-start.8 = (bf16[2,32,1280]{2,1,0:T(8,128)(2,1)S(1)}, bf16[2,32,1280]{2,1,0:T(8,128)(2,1)S(1)}, u32[]{:S(2)}, u32[]{:S(2)}) collective-permute-start(bf16[2,32,1280]{2,1,0:T(8,128)(2,1)S(1)} %collective-permute-done.7.refs_6_), channel_id=1, source_target_pairs={{0,24},{8,0},{16,8},{24,16},{32,56},{40,32},{48,40},{56,48},{64,88... | collective-permute-start | bytes 491528 | tf_op jit(solution)/shard_map/ppermute | solution.py:43
  144.1 55.2 %all-to-all-start.1 = ((bf16[16,4,2,128,128]{4,3,2,1,0:T(8,128)(2,1)}), bf16[16,4,2,128,128]{4,3,2,1,0:T(8,128)(2,1)}, u32[]{:S(2)}, u32[]{:S(2)}) async-start(bf16[16,4,2,128,128]{4,3,2,1,0:T(8,128)(2,1)} %write_tokens.1), calls=%async_computation.1 | async-start | bytes 8388608 | tf_op jit(solution)/shard_map/all_to_all | solution.py:499
  149.6 40.2 %copy-start.10 = (s32[640]{0:T(1024)S(1)}, s32[640]{0:T(1024)}, u32[]{:S(2)}) copy-start(s32[640]{0:T(1024)} %copy-done.9) | copy-start | bytes 7684
  152.0 6.8 %collective-permute-start.9 = (f32[64,512]{1,0:T(8,128)S(1)}, f32[64,512]{1,0:T(8,128)S(1)}, u32[]{:S(2)}, u32[]{:S(2)}) collective-permute-start(f32[64,512]{1,0:T(8,128)S(1)} %get-tuple-element.16), channel_id=1, source_target_pairs={{0,1},{1,0},{2,3},{3,2},{4,5},{5,4},{6,7},{7,6},{8,9},{9,8},{10,11... | collective-permute-start | bytes 393224 | tf_op jit(solution)/shard_map/ppermute | solution.py:55
  152.0 8.4 %collective-permute-start.10 = (f32[64,512]{1,0:T(8,128)S(1)}, f32[64,512]{1,0:T(8,128)S(1)}, u32[]{:S(2)}, u32[]{:S(2)}) collective-permute-start(f32[64,512]{1,0:T(8,128)S(1)} %get-tuple-element.17), channel_id=1, source_target_pairs={{0,2},{1,3},{2,4},{3,5},{4,6},{5,7},{6,0},{7,1},{8,10},{9,11},{10,... | collective-permute-start | bytes 393224 | tf_op jit(solution)/shard_map/ppermute | solution.py:55
  153.9 8.9 %collective-permute-start.11 = (f32[64,512]{1,0:T(8,128)S(1)}, f32[64,512]{1,0:T(8,128)S(1)}, u32[]{:S(2)}, u32[]{:S(2)}) collective-permute-start(f32[64,512]{1,0:T(8,128)S(1)} %get-tuple-element.18), channel_id=1, source_target_pairs={{0,3},{1,2},{2,5},{3,4},{4,7},{5,6},{6,1},{7,0},{8,11},{9,10},{10,... | collective-permute-start | bytes 393224 | tf_op jit(solution)/shard_map/ppermute | solution.py:55
  155.7 11.7 %collective-permute-start.12 = (f32[64,512]{1,0:T(8,128)S(1)}, f32[64,512]{1,0:T(8,128)S(1)}, u32[]{:S(2)}, u32[]{:S(2)}) collective-permute-start(f32[64,512]{1,0:T(8,128)S(1)} %get-tuple-element.19), channel_id=1, source_target_pairs={{0,4},{1,5},{2,6},{3,7},{4,0},{5,1},{6,2},{7,3},{8,12},{9,13},{10,... | collective-permute-start | bytes 393224 | tf_op jit(solution)/shard_map/ppermute | solution.py:55
  157.7 11.8 %collective-permute-start.13 = (f32[64,512]{1,0:T(8,128)S(1)}, f32[64,512]{1,0:T(8,128)S(1)}, u32[]{:S(2)}, u32[]{:S(2)}) collective-permute-start(f32[64,512]{1,0:T(8,128)S(1)} %get-tuple-element.20), channel_id=1, source_target_pairs={{0,5},{1,4},{2,7},{3,6},{4,1},{5,0},{6,3},{7,2},{8,13},{9,12},{10,... | collective-permute-start | bytes 393224 | tf_op jit(solution)/shard_map/ppermute | solution.py:55
  158.9 11.2 %copy-start.13 = (f32[64,512]{1,0:T(8,128)}, f32[64,512]{1,0:T(8,128)S(1)}, u32[]{:S(2)}) copy-start(f32[64,512]{1,0:T(8,128)S(1)} %collective-permute-done.9.refs_1_) | copy-start | bytes 393220
  158.9 10.6 %collective-permute-start.14 = (f32[64,512]{1,0:T(8,128)S(1)}, f32[64,512]{1,0:T(8,128)S(1)}, u32[]{:S(2)}, u32[]{:S(2)}) collective-permute-start(f32[64,512]{1,0:T(8,128)S(1)} %get-tuple-element.21), channel_id=1, source_target_pairs={{0,6},{1,7},{2,0},{3,1},{4,2},{5,3},{6,4},{7,5},{8,14},{9,15},{10,... | collective-permute-start | bytes 393224 | tf_op jit(solution)/shard_map/ppermute | solution.py:55
  160.4 9.7 %copy-start.14 = (f32[64,512]{1,0:T(8,128)}, f32[64,512]{1,0:T(8,128)S(1)}, u32[]{:S(2)}) copy-start(f32[64,512]{1,0:T(8,128)S(1)} %collective-permute-done.10.refs_2_) | copy-start | bytes 393220
  160.4 9.7 %collective-permute-start.15 = (f32[64,512]{1,0:T(8,128)S(1)}, f32[64,512]{1,0:T(8,128)S(1)}, u32[]{:S(2)}, u32[]{:S(2)}) collective-permute-start(f32[64,512]{1,0:T(8,128)S(1)} %get-tuple-element.22), channel_id=1, source_target_pairs={{0,7},{1,6},{2,1},{3,0},{4,3},{5,2},{6,5},{7,4},{8,15},{9,14},{10,... | collective-permute-start | bytes 393224 | tf_op jit(solution)/shard_map/ppermute | solution.py:55
  172.7 7.6 %collective-permute-start.22 = (bf16[64,512]{1,0:T(8,128)(2,1)}, bf16[64,512]{1,0:T(8,128)(2,1)S(1)}, u32[]{:S(2)}, u32[]{:S(2)}) collective-permute-start(bf16[64,512]{1,0:T(8,128)(2,1)} %total_rows.1.refs_0_), channel_id=1, source_target_pairs={{0,7},{1,6},{2,1},{3,0},{4,3},{5,2},{6,5},{7,4},{8,15},{9,14},{10,... | collective-permute-start | bytes 196616 | tf_op jit(solution)/shard_map/ppermute | solution.py:55
  175.3 5.2 %collective-permute-start.21 = (bf16[64,512]{1,0:T(8,128)(2,1)}, bf16[64,512]{1,0:T(8,128)(2,1)S(1)}, u32[]{:S(2)}, u32[]{:S(2)}) collective-permute-start(bf16[64,512]{1,0:T(8,128)(2,1)} %total_rows.1.refs_0_), channel_id=1, source_target_pairs={{0,6},{1,7},{2,0},{3,1},{4,2},{5,3},{6,4},{7,5},{8,14},{9,15},{10,... | collective-permute-start | bytes 196616 | tf_op jit(solution)/shard_map/ppermute | solution.py:55
  176.6 5.7 %collective-permute-start.20 = (bf16[64,512]{1,0:T(8,128)(2,1)}, bf16[64,512]{1,0:T(8,128)(2,1)S(1)}, u32[]{:S(2)}, u32[]{:S(2)}) collective-permute-start(bf16[64,512]{1,0:T(8,128)(2,1)} %total_rows.1.refs_0_), channel_id=1, source_target_pairs={{0,5},{1,4},{2,7},{3,6},{4,1},{5,0},{6,3},{7,2},{8,13},{9,12},{10,... | collective-permute-start | bytes 196616 | tf_op jit(solution)/shard_map/ppermute | solution.py:55
  177.3 6.4 %collective-permute-start.19 = (bf16[64,512]{1,0:T(8,128)(2,1)}, bf16[64,512]{1,0:T(8,128)(2,1)S(1)}, u32[]{:S(2)}, u32[]{:S(2)}) collective-permute-start(bf16[64,512]{1,0:T(8,128)(2,1)} %total_rows.1.refs_0_), channel_id=1, source_target_pairs={{0,4},{1,5},{2,6},{3,7},{4,0},{5,1},{6,2},{7,3},{8,12},{9,13},{10,... | collective-permute-start | bytes 196616 | tf_op jit(solution)/shard_map/ppermute | solution.py:55
  179.1 5.3 %collective-permute-start.18 = (bf16[64,512]{1,0:T(8,128)(2,1)}, bf16[64,512]{1,0:T(8,128)(2,1)S(1)}, u32[]{:S(2)}, u32[]{:S(2)}) collective-permute-start(bf16[64,512]{1,0:T(8,128)(2,1)} %total_rows.1.refs_0_), channel_id=1, source_target_pairs={{0,3},{1,2},{2,5},{3,4},{4,7},{5,6},{6,1},{7,0},{8,11},{9,10},{10,... | collective-permute-start | bytes 196616 | tf_op jit(solution)/shard_map/ppermute | solution.py:55
  180.3 6.3 %collective-permute-start.17 = (bf16[64,512]{1,0:T(8,128)(2,1)}, bf16[64,512]{1,0:T(8,128)(2,1)S(1)}, u32[]{:S(2)}, u32[]{:S(2)}) collective-permute-start(bf16[64,512]{1,0:T(8,128)(2,1)} %total_rows.1.refs_0_), channel_id=1, source_target_pairs={{0,2},{1,3},{2,4},{3,5},{4,6},{5,7},{6,0},{7,1},{8,10},{9,11},{10,... | collective-permute-start | bytes 196616 | tf_op jit(solution)/shard_map/ppermute | solution.py:55
  180.6 6.1 %collective-permute-start.16 = (bf16[64,512]{1,0:T(8,128)(2,1)}, bf16[64,512]{1,0:T(8,128)(2,1)S(1)}, u32[]{:S(2)}, u32[]{:S(2)}) collective-permute-start(bf16[64,512]{1,0:T(8,128)(2,1)} %total_rows.1.refs_0_), channel_id=1, source_target_pairs={{0,1},{1,0},{2,3},{3,2},{4,5},{5,4},{6,7},{7,6},{8,9},{9,8},{10,11... | collective-permute-start | bytes 196616 | tf_op jit(solution)/shard_map/ppermute | solution.py:55
  (24 other events, 65.4 us)

commit v4 on v3

--- a/solution.py
+++ b/solution.py
@@ -511,6 +511,7 @@
     near = exchange(lax.optimization_barrier((near, sums))[0])
     mine, new = attend(ints, sums, kv_pool)
     far = write_tokens(CUTS[1], ints, new, far)
+    mine, far = lax.optimization_barrier((mine, far))
     line = steps_back(mine, 1, 0)
     pieces = steps_back(jnp.stack(line[:2]), 0, 1) + steps_back(jnp.stack(line[2:]), 0, 1)
     far = exchange(lax.optimization_barrier((far, pieces))[0])

time: 204 us -> 202 us (level)
  local copies, waits for them, and re-layouts: 16.8 us -> 14.7 us
    ppermute x9, waiting for transfers between devices: 57.6 us -> 55.1 us  [move(): return lax.ppermute(array, 'grp', pairs)]
    unnamed x60, local copies, waits for them, and re-layouts: 16 us -> 14 us
  transfers between devices with their start and end apart: 26 -> 26, of which waited for: 18 -> 20; matrix products, arithmetic and copies ran while one was open for 0% -> 0% of each run, Pallas kernels for 13% -> 13%
where the time goes in v4:
time: 202 us; the launch traced here: 201 us
  waiting for transfers between devices  111 us (55%)
  starting transfers between devices  44.9 us (22%)
  Pallas kernels  30 us (15%)
  local copies, waits for them, and re-layouts  14.7 us (7%)
    ppermute x9, waiting for transfers between devices, move(): return lax.ppermute(array, 'grp', pairs)  55.1 us
    all_to_all x3, waiting for transfers between devices, exchange(): return lax.all_to_all(array, 'grp', split_axis=0, concat_axis=0, tiled=True)  40.5 us
    all_to_all x3, starting transfers between devices, exchange(): return lax.all_to_all(array, 'grp', split_axis=0, concat_axis=0, tiled=True)  17.7 us
    ppermute x14, starting transfers between devices, move_part(): return lax.ppermute(array, 'tp', pairs)  17 us
    ppermute x14, waiting for transfers between devices, move_part(): return lax.ppermute(array, 'tp', pairs)  14.9 us
    unnamed x60, local copies, waits for them, and re-layouts  14 us
    ppermute x9, starting transfers between devices, move(): return lax.ppermute(array, 'grp', pairs)  10.2 us
    pallas_call x2, Pallas kernels, gather_pages(): pl.pallas_call(functools.partial(gather_kernel, low), out_shape=shape, in...  6.26 us
  transfers between devices with their start and end apart: 26, of which 20 were waited for; matrix products, arithmetic and copies ran while one was open for 0% of the time, Pallas kernels for 13%

profile of v4, /device:TPU:0, one launch (start us, length us, event | category | flops | bytes accessed | tf_op | source)
XLA Modules:
  0.0 201.1 jit_solution(8387489102143727061)
XLA Ops:
  6.1 7.1 %all-to-all-start = ((f32[16,328,128]{2,1,0:T(8,128)}), f32[16,328,128]{2,1,0:T(8,128)S(1)}, u32[]{:S(2)}, u32[]{:S(2)}) async-start(f32[16,328,128]{2,1,0:T(8,128)} %copy-done.3), calls=%async_computation | async-start | bytes 5373952 | tf_op jit(solution)/shard_map/all_to_all | solution.py:499
  13.3 3.3 %gather_pages.3 = bf16[16,4,2,128,128]{4,3,2,1,0:T(8,128)(2,1)S(1)} custom-call(s32[640]{0:T(1024)S(1)} %pad_add_fusion.ints_ref, bf16[128,2,1,128,128]{4,3,2,1,0:T(8,128)(2,1)} %pool_ref.3), custom_call_target="tpu_custom_call" | custom-call | bytes 8388608 | tf_op jit(solution)/shard_map/gather_pages/pallas_call | solution.py:137
  16.6 2.0 copy-done.2
  18.6 35.2 %all-to-all-done.refs_0_ = f32[16,328,128]{2,1,0:T(8,128)S(1)} async-done(((f32[16,328,128]{2,1,0:T(8,128)}), f32[16,328,128]{2,1,0:T(8,128)S(1)}, u32[]{:S(2)}, u32[]{:S(2)}) %all-to-all-start) | async-done | bytes 2687008 | tf_op jit(solution)/shard_map/all_to_all | solution.py:499
  53.9 4.6 %all-to-all-start.2 = ((bf16[16,4,2,128,128]{4,3,2,1,0:T(8,128)(2,1)}), bf16[16,4,2,128,128]{4,3,2,1,0:T(8,128)(2,1)}, u32[]{:S(2)}, u32[]{:S(2)}) async-start(bf16[16,4,2,128,128]{4,3,2,1,0:T(8,128)(2,1)} %copy-done.2), calls=%async_computation.2 | async-start | bytes 8388608 | tf_op jit(solution)/shard_map/all_to_all | solution.py:499
  58.4 2.9 %gather_pages.2.pages_in = bf16[16,4,2,128,128]{4,3,2,1,0:T(8,128)(2,1)S(1)} custom-call(s32[640]{0:T(1024)S(1)} %pad_add_fusion.ints_ref, bf16[128,2,1,128,128]{4,3,2,1,0:T(8,128)(2,1)} %pool_ref.3), custom_call_target="tpu_custom_call" | custom-call | bytes 8388608 | tf_op jit(solution)/shard_map/gather_pages/pallas_call | solution.py:137
  61.4 3.4 %copy-done = bf16[128,2,1,128,128]{4,3,2,1,0:T(8,128)(2,1)S(1)} copy-done((bf16[128,2,1,128,128]{4,3,2,1,0:T(8,128)(2,1)S(1)}, bf16[128,2,1,128,128]{4,3,2,1,0:T(8,128)(2,1)}, u32[]{:S(2)}) %copy-start) | copy-done | bytes 8388632
  64.8 4.7 %attend.1 = (bf16[32,1280]{1,0:T(8,128)(2,1)S(1)}, f32[2,32,128]{2,1,0:T(8,128)S(1)}) custom-call(s32[640]{0:T(1024)S(1)} %pad_add_fusion.ints_ref, f32[16,328,128]{2,1,0:T(8,128)S(1)} %all-to-all-done.refs_0_, bf16[128,2,1,128,128]{4,3,2,1,0:T(8,128)(2,1)S(1)} %copy-done), custom_call_target="tpu_custom_call" | custom-call | flops 134217728 | bytes 10485760 | tf_op jit(solution)/shard_map/attend/pallas_call | solution.py:230
  70.1 3.3 %write_tokens.1 = bf16[16,4,2,128,128]{4,3,2,1,0:T(8,128)(2,1)} custom-call(s32[640]{0:T(1024)} %copy-done.9, f32[2,32,128]{2,1,0:T(8,128)} %copy-done.12, bf16[16,4,2,128,128]{4,3,2,1,0:T(8,128)(2,1)} %copy-done.1), custom_call_target="tpu_custom_call", output_to_operand_aliasing={{}: (2, {})} | custom-call | bytes 1048576 | tf_op jit(solution)/shard_map/write_tokens/pallas_call | solution.py:458
  73.5 3.1 %collective-permute-start = (bf16[32,1280]{1,0:T(8,128)(2,1)S(1)}, bf16[32,1280]{1,0:T(8,128)(2,1)S(1)}, u32[]{:S(2)}, u32[]{:S(2)}) collective-permute-start(bf16[32,1280]{1,0:T(8,128)(2,1)S(1)} %get-tuple-element.18), channel_id=1, source_target_pairs={{0,96},{8,104},{16,112},{24,120},{32,0},{40,8},{48,16},{56,24},{64... | collective-permute-start | bytes 245768 | tf_op jit(solution)/shard_map/ppermute | solution.py:43
  76.6 30.4 %collective-permute-done = bf16[32,1280]{1,0:T(8,128)(2,1)S(1)} collective-permute-done((bf16[32,1280]{1,0:T(8,128)(2,1)S(1)}, bf16[32,1280]{1,0:T(8,128)(2,1)S(1)}, u32[]{:S(2)}, u32[]{:S(2)}) %collective-permute-start) | collective-permute-done | bytes 81952 | tf_op jit(solution)/shard_map/ppermute | solution.py:43
  107.0 4.8 %collective-permute-done.4 = bf16[32,1280]{1,0:T(8,128)(2,1)S(1)} collective-permute-done((bf16[32,1280]{1,0:T(8,128)(2,1)S(1)}, bf16[32,1280]{1,0:T(8,128)(2,1)S(1)}, u32[]{:S(2)}, u32[]{:S(2)}) %collective-permute-start.4) | collective-permute-done | bytes 81952 | tf_op jit(solution)/shard_map/ppermute | solution.py:43
  114.4 1.9 collective-permute-done.5
  117.1 5.7 %collective-permute-done.1.refs_1_ = bf16[2,32,1280]{2,1,0:T(8,128)(2,1)S(1)} collective-permute-done((bf16[2,32,1280]{2,1,0:T(8,128)(2,1)S(1)}, bf16[2,32,1280]{2,1,0:T(8,128)(2,1)S(1)}, u32[]{:S(2)}, u32[]{:S(2)}) %collective-permute-start.1) | collective-permute-done | bytes 163872 | tf_op jit(solution)/shard_map/ppermute | solution.py:43
  123.8 2.5 %collective-permute-done.6.refs_5_ = bf16[2,32,1280]{2,1,0:T(8,128)(2,1)S(1)} collective-permute-done((bf16[2,32,1280]{2,1,0:T(8,128)(2,1)S(1)}, bf16[2,32,1280]{2,1,0:T(8,128)(2,1)S(1)}, u32[]{:S(2)}, u32[]{:S(2)}) %collective-permute-start.6) | collective-permute-done | bytes 163872 | tf_op jit(solution)/shard_map/ppermute | solution.py:43
  127.2 2.8 %collective-permute-done.2.refs_2_ = bf16[2,32,1280]{2,1,0:T(8,128)(2,1)S(1)} collective-permute-done((bf16[2,32,1280]{2,1,0:T(8,128)(2,1)S(1)}, bf16[2,32,1280]{2,1,0:T(8,128)(2,1)S(1)}, u32[]{:S(2)}, u32[]{:S(2)}) %collective-permute-start.2) | collective-permute-done | bytes 163872 | tf_op jit(solution)/shard_map/ppermute | solution.py:43
  130.6 2.9 %collective-permute-done.7.refs_6_ = bf16[2,32,1280]{2,1,0:T(8,128)(2,1)S(1)} collective-permute-done((bf16[2,32,1280]{2,1,0:T(8,128)(2,1)S(1)}, bf16[2,32,1280]{2,1,0:T(8,128)(2,1)S(1)}, u32[]{:S(2)}, u32[]{:S(2)}) %collective-permute-start.7) | collective-permute-done | bytes 163872 | tf_op jit(solution)/shard_map/ppermute | solution.py:43
  136.4 2.5 %collective-permute-done.8.refs_7_ = bf16[2,32,1280]{2,1,0:T(8,128)(2,1)S(1)} collective-permute-done((bf16[2,32,1280]{2,1,0:T(8,128)(2,1)S(1)}, bf16[2,32,1280]{2,1,0:T(8,128)(2,1)S(1)}, u32[]{:S(2)}, u32[]{:S(2)}) %collective-permute-start.8) | collective-permute-done | bytes 163872 | tf_op jit(solution)/shard_map/ppermute | solution.py:43
  139.5 6.0 %all-to-all-start.1 = ((bf16[16,4,2,128,128]{4,3,2,1,0:T(8,128)(2,1)}), bf16[16,4,2,128,128]{4,3,2,1,0:T(8,128)(2,1)}, u32[]{:S(2)}, u32[]{:S(2)}) async-start(bf16[16,4,2,128,128]{4,3,2,1,0:T(8,128)(2,1)} %write_tokens.1), calls=%async_computation.1 | async-start | bytes 8388608 | tf_op jit(solution)/shard_map/all_to_all | solution.py:499
  148.8 1.9 collective-permute-start.10
  150.8 1.8 collective-permute-start.11
  152.5 1.9 collective-permute-start.12
  159.7 4.6 %collective-permute-done.12.refs_4_ = f32[64,512]{1,0:T(8,128)S(1)} collective-permute-done((f32[64,512]{1,0:T(8,128)S(1)}, f32[64,512]{1,0:T(8,128)S(1)}, u32[]{:S(2)}, u32[]{:S(2)}) %collective-permute-start.12) | collective-permute-done | bytes 131104 | tf_op jit(solution)/shard_map/ppermute | solution.py:55
  164.2 2.0 %collective-permute-done.13.refs_5_ = f32[64,512]{1,0:T(8,128)S(1)} collective-permute-done((f32[64,512]{1,0:T(8,128)S(1)}, f32[64,512]{1,0:T(8,128)S(1)}, u32[]{:S(2)}, u32[]{:S(2)}) %collective-permute-start.13) | collective-permute-done | bytes 131104 | tf_op jit(solution)/shard_map/ppermute | solution.py:55
  167.6 2.0 total_rows.1.refs_0_
  169.5 2.6 %collective-permute-start.22 = (bf16[64,512]{1,0:T(8,128)(2,1)}, bf16[64,512]{1,0:T(8,128)(2,1)S(1)}, u32[]{:S(2)}, u32[]{:S(2)}) collective-permute-start(bf16[64,512]{1,0:T(8,128)(2,1)} %total_rows.1.refs_0_), channel_id=1, source_target_pairs={{0,7},{1,6},{2,1},{3,0},{4,3},{5,2},{6,5},{7,4},{8,15},{9,14},{10,... | collective-permute-start | bytes 196616 | tf_op jit(solution)/shard_map/ppermute | solution.py:55
  174.1 1.8 collective-permute-start.19
  181.2 2.3 %collective-permute-done.17.refs_2_ = bf16[64,512]{1,0:T(8,128)(2,1)S(1)} collective-permute-done((bf16[64,512]{1,0:T(8,128)(2,1)}, bf16[64,512]{1,0:T(8,128)(2,1)S(1)}, u32[]{:S(2)}, u32[]{:S(2)}) %collective-permute-start.17) | collective-permute-done | bytes 65568 | tf_op jit(solution)/shard_map/ppermute | solution.py:55
  184.7 1.9 order_rows.1
  186.6 5.4 %insert_tokens.1.cache_in = bf16[16,8,2,1,128,128]{5,4,3,2,1,0:T(8,128)(2,1)} custom-call(s32[640]{0:T(1024)S(1)} %copy-done.10, bf16[16,32,1280]{2,1,0:T(8,128)(2,1)S(1)} %arrange.1.rows_ref, bf16[16,4,2,128,128]{4,3,2,1,0:T(8,128)(2,1)} %all-to-all-done.2.pages_ref), custom_call_target="tpu_custom_call" | custom-call | bytes 8388608 | tf_op jit(solution)/shard_map/insert_tokens/pallas_call | solution.py:389
  192.0 5.3 %all-to-all-done.1.pages_ref = bf16[16,4,2,128,128]{4,3,2,1,0:T(8,128)(2,1)} async-done(((bf16[16,4,2,128,128]{4,3,2,1,0:T(8,128)(2,1)}), bf16[16,4,2,128,128]{4,3,2,1,0:T(8,128)(2,1)}, u32[]{:S(2)}, u32[]{:S(2)}) %all-to-all-start.1) | async-done | bytes 4194336 | tf_op jit(solution)/shard_map/all_to_all | solution.py:499
  197.3 3.8 %settle.1 = bf16[16,8,2,1,128,128]{5,4,3,2,1,0:T(8,128)(2,1)} custom-call(bf16[16,4,2,128,128]{4,3,2,1,0:T(8,128)(2,1)} %all-to-all-done.1.pages_ref, bf16[16,8,2,1,128,128]{5,4,3,2,1,0:T(8,128)(2,1)} %insert_tokens.1.cache_in), custom_call_target="tpu_custom_call", output_to_operand_aliasing={{}: (1, {})} | custom-call | bytes 8388608 | tf_op jit(solution)/shard_map/settle/pallas_call | solution.py:485
  (96 shorter events, 33.6 us)
Async XLA Ops:
  3.7 9.6 %copy-start.29 = (s32[1,128]{1,0:T(1,128)S(1)}, s32[1,128]{1,0:T(1,128)}, u32[]{:S(2)}) copy-start(s32[1,128]{1,0:T(1,128)} %param.10) | copy-start | bytes 1540
  6.1 47.8 %all-to-all-start = ((f32[16,328,128]{2,1,0:T(8,128)}), f32[16,328,128]{2,1,0:T(8,128)S(1)}, u32[]{:S(2)}, u32[]{:S(2)}) async-start(f32[16,328,128]{2,1,0:T(8,128)} %copy-done.3), calls=%async_computation | async-start | bytes 5373952 | tf_op jit(solution)/shard_map/all_to_all | solution.py:499
  13.3 48.1 %copy-start.9 = (s32[640]{0:T(1024)}, s32[640]{0:T(1024)S(1)}, u32[]{:S(2)}) copy-start(s32[640]{0:T(1024)S(1)} %pad_add_fusion.ints_ref) | copy-start | bytes 7684
  53.9 85.6 %all-to-all-start.2 = ((bf16[16,4,2,128,128]{4,3,2,1,0:T(8,128)(2,1)}), bf16[16,4,2,128,128]{4,3,2,1,0:T(8,128)(2,1)}, u32[]{:S(2)}, u32[]{:S(2)}) async-start(bf16[16,4,2,128,128]{4,3,2,1,0:T(8,128)(2,1)} %copy-done.2), calls=%async_computation.2 | async-start | bytes 8388608 | tf_op jit(solution)/shard_map/all_to_all | solution.py:499
  73.5 33.6 %collective-permute-start = (bf16[32,1280]{1,0:T(8,128)(2,1)S(1)}, bf16[32,1280]{1,0:T(8,128)(2,1)S(1)}, u32[]{:S(2)}, u32[]{:S(2)}) collective-permute-start(bf16[32,1280]{1,0:T(8,128)(2,1)S(1)} %get-tuple-element.18), channel_id=1, source_target_pairs={{0,96},{8,104},{16,112},{24,120},{32,0},{40,8},{48,16},{56,24},{64... | collective-permute-start | bytes 245768 | tf_op jit(solution)/shard_map/ppermute | solution.py:43
  107.0 4.8 %collective-permute-start.4 = (bf16[32,1280]{1,0:T(8,128)(2,1)S(1)}, bf16[32,1280]{1,0:T(8,128)(2,1)S(1)}, u32[]{:S(2)}, u32[]{:S(2)}) collective-permute-start(bf16[32,1280]{1,0:T(8,128)(2,1)S(1)} %collective-permute-done), channel_id=1, source_target_pairs={{0,96},{8,104},{16,112},{24,120},{32,0},{40,8},{48,16},{56,24},{64... | collective-permute-start | bytes 245768 | tf_op jit(solution)/shard_map/ppermute | solution.py:43
  111.9 4.4 %collective-permute-start.5 = (bf16[32,1280]{1,0:T(8,128)(2,1)S(1)}, bf16[32,1280]{1,0:T(8,128)(2,1)S(1)}, u32[]{:S(2)}, u32[]{:S(2)}) collective-permute-start(bf16[32,1280]{1,0:T(8,128)(2,1)S(1)} %collective-permute-done.4), channel_id=1, source_target_pairs={{0,96},{8,104},{16,112},{24,120},{32,0},{40,8},{48,16},{56,24},{64... | collective-permute-start | bytes 245768 | tf_op jit(solution)/shard_map/ppermute | solution.py:43
  113.5 9.3 %collective-permute-start.1 = (bf16[2,32,1280]{2,1,0:T(8,128)(2,1)S(1)}, bf16[2,32,1280]{2,1,0:T(8,128)(2,1)S(1)}, u32[]{:S(2)}, u32[]{:S(2)}) collective-permute-start(bf16[2,32,1280]{2,1,0:T(8,128)(2,1)S(1)} %pad_maximum_fusion.refs_0_), channel_id=1, source_target_pairs={{0,24},{8,0},{16,8},{24,16},{32,56},{40,32},{48,40},{56,48},{64,88... | collective-permute-start | bytes 491528 | tf_op jit(solution)/shard_map/ppermute | solution.py:43
  116.3 30.2 %copy-start.5 = (bf16[1,1024,512]{2,1,0:T(8,128)(2,1)S(1)}, bf16[1,1024,512]{2,1,0:T(8,128)(2,1)}, u32[]{:S(2)}) copy-start(bf16[1,1024,512]{2,1,0:T(8,128)(2,1)} %param.15) | copy-start | bytes 3145732
  116.3 10.0 %collective-permute-start.6 = (bf16[2,32,1280]{2,1,0:T(8,128)(2,1)S(1)}, bf16[2,32,1280]{2,1,0:T(8,128)(2,1)S(1)}, u32[]{:S(2)}, u32[]{:S(2)}) collective-permute-start(bf16[2,32,1280]{2,1,0:T(8,128)(2,1)S(1)} %pad_maximum_fusion.1.refs_4_), channel_id=1, source_target_pairs={{0,24},{8,0},{16,8},{24,16},{32,56},{40,32},{48,40},{56,48},{64,88... | collective-permute-start | bytes 491528 | tf_op jit(solution)/shard_map/ppermute | solution.py:43
  122.9 7.1 %collective-permute-start.2 = (bf16[2,32,1280]{2,1,0:T(8,128)(2,1)S(1)}, bf16[2,32,1280]{2,1,0:T(8,128)(2,1)S(1)}, u32[]{:S(2)}, u32[]{:S(2)}) collective-permute-start(bf16[2,32,1280]{2,1,0:T(8,128)(2,1)S(1)} %collective-permute-done.1.refs_1_), channel_id=1, source_target_pairs={{0,24},{8,0},{16,8},{24,16},{32,56},{40,32},{48,40},{56,48},{64,88... | collective-permute-start | bytes 491528 | tf_op jit(solution)/shard_map/ppermute | solution.py:43
  126.4 7.1 %collective-permute-start.7 = (bf16[2,32,1280]{2,1,0:T(8,128)(2,1)S(1)}, bf16[2,32,1280]{2,1,0:T(8,128)(2,1)S(1)}, u32[]{:S(2)}, u32[]{:S(2)}) collective-permute-start(bf16[2,32,1280]{2,1,0:T(8,128)(2,1)S(1)} %collective-permute-done.6.refs_5_), channel_id=1, source_target_pairs={{0,24},{8,0},{16,8},{24,16},{32,56},{40,32},{48,40},{56,48},{64,88... | collective-permute-start | bytes 491528 | tf_op jit(solution)/shard_map/ppermute | solution.py:43
  130.0 6.4 %collective-permute-start.3 = (bf16[2,32,1280]{2,1,0:T(8,128)(2,1)S(1)}, bf16[2,32,1280]{2,1,0:T(8,128)(2,1)S(1)}, u32[]{:S(2)}, u32[]{:S(2)}) collective-permute-start(bf16[2,32,1280]{2,1,0:T(8,128)(2,1)S(1)} %collective-permute-done.2.refs_2_), channel_id=1, source_target_pairs={{0,24},{8,0},{16,8},{24,16},{32,56},{40,32},{48,40},{56,48},{64,88... | collective-permute-start | bytes 491528 | tf_op jit(solution)/shard_map/ppermute | solution.py:43
  133.5 5.3 %collective-permute-start.8 = (bf16[2,32,1280]{2,1,0:T(8,128)(2,1)S(1)}, bf16[2,32,1280]{2,1,0:T(8,128)(2,1)S(1)}, u32[]{:S(2)}, u32[]{:S(2)}) collective-permute-start(bf16[2,32,1280]{2,1,0:T(8,128)(2,1)S(1)} %collective-permute-done.7.refs_6_), channel_id=1, source_target_pairs={{0,24},{8,0},{16,8},{24,16},{32,56},{40,32},{48,40},{56,48},{64,88... | collective-permute-start | bytes 491528 | tf_op jit(solution)/shard_map/ppermute | solution.py:43
  139.5 57.8 %all-to-all-start.1 = ((bf16[16,4,2,128,128]{4,3,2,1,0:T(8,128)(2,1)}), bf16[16,4,2,128,128]{4,3,2,1,0:T(8,128)(2,1)}, u32[]{:S(2)}, u32[]{:S(2)}) async-start(bf16[16,4,2,128,128]{4,3,2,1,0:T(8,128)(2,1)} %write_tokens.1), calls=%async_computation.1 | async-start | bytes 8388608 | tf_op jit(solution)/shard_map/all_to_all | solution.py:499
  146.4 40.2 %copy-start.10 = (s32[640]{0:T(1024)S(1)}, s32[640]{0:T(1024)}, u32[]{:S(2)}) copy-start(s32[640]{0:T(1024)} %copy-done.9) | copy-start | bytes 7684
  148.8 6.8 %collective-permute-start.9 = (f32[64,512]{1,0:T(8,128)S(1)}, f32[64,512]{1,0:T(8,128)S(1)}, u32[]{:S(2)}, u32[]{:S(2)}) collective-permute-start(f32[64,512]{1,0:T(8,128)S(1)} %get-tuple-element.20), channel_id=1, source_target_pairs={{0,1},{1,0},{2,3},{3,2},{4,5},{5,4},{6,7},{7,6},{8,9},{9,8},{10,11... | collective-permute-start | bytes 393224 | tf_op jit(solution)/shard_map/ppermute | solution.py:55
  148.8 8.4 %collective-permute-start.10 = (f32[64,512]{1,0:T(8,128)S(1)}, f32[64,512]{1,0:T(8,128)S(1)}, u32[]{:S(2)}, u32[]{:S(2)}) collective-permute-start(f32[64,512]{1,0:T(8,128)S(1)} %get-tuple-element.21), channel_id=1, source_target_pairs={{0,2},{1,3},{2,4},{3,5},{4,6},{5,7},{6,0},{7,1},{8,10},{9,11},{10,... | collective-permute-start | bytes 393224 | tf_op jit(solution)/shard_map/ppermute | solution.py:55
  150.8 8.9 %collective-permute-start.11 = (f32[64,512]{1,0:T(8,128)S(1)}, f32[64,512]{1,0:T(8,128)S(1)}, u32[]{:S(2)}, u32[]{:S(2)}) collective-permute-start(f32[64,512]{1,0:T(8,128)S(1)} %get-tuple-element.22), channel_id=1, source_target_pairs={{0,3},{1,2},{2,5},{3,4},{4,7},{5,6},{6,1},{7,0},{8,11},{9,10},{10,... | collective-permute-start | bytes 393224 | tf_op jit(solution)/shard_map/ppermute | solution.py:55
  152.5 11.7 %collective-permute-start.12 = (f32[64,512]{1,0:T(8,128)S(1)}, f32[64,512]{1,0:T(8,128)S(1)}, u32[]{:S(2)}, u32[]{:S(2)}) collective-permute-start(f32[64,512]{1,0:T(8,128)S(1)} %get-tuple-element.23), channel_id=1, source_target_pairs={{0,4},{1,5},{2,6},{3,7},{4,0},{5,1},{6,2},{7,3},{8,12},{9,13},{10,... | collective-permute-start | bytes 393224 | tf_op jit(solution)/shard_map/ppermute | solution.py:55
  154.5 11.8 %collective-permute-start.13 = (f32[64,512]{1,0:T(8,128)S(1)}, f32[64,512]{1,0:T(8,128)S(1)}, u32[]{:S(2)}, u32[]{:S(2)}) collective-permute-start(f32[64,512]{1,0:T(8,128)S(1)} %get-tuple-element.24), channel_id=1, source_target_pairs={{0,5},{1,4},{2,7},{3,6},{4,1},{5,0},{6,3},{7,2},{8,13},{9,12},{10,... | collective-permute-start | bytes 393224 | tf_op jit(solution)/shard_map/ppermute | solution.py:55
  155.7 11.2 %copy-start.13 = (f32[64,512]{1,0:T(8,128)}, f32[64,512]{1,0:T(8,128)S(1)}, u32[]{:S(2)}) copy-start(f32[64,512]{1,0:T(8,128)S(1)} %collective-permute-done.9.refs_1_) | copy-start | bytes 393220
  155.7 10.6 %collective-permute-start.14 = (f32[64,512]{1,0:T(8,128)S(1)}, f32[64,512]{1,0:T(8,128)S(1)}, u32[]{:S(2)}, u32[]{:S(2)}) collective-permute-start(f32[64,512]{1,0:T(8,128)S(1)} %get-tuple-element.25), channel_id=1, source_target_pairs={{0,6},{1,7},{2,0},{3,1},{4,2},{5,3},{6,4},{7,5},{8,14},{9,15},{10,... | collective-permute-start | bytes 393224 | tf_op jit(solution)/shard_map/ppermute | solution.py:55
  157.2 9.7 %copy-start.14 = (f32[64,512]{1,0:T(8,128)}, f32[64,512]{1,0:T(8,128)S(1)}, u32[]{:S(2)}) copy-start(f32[64,512]{1,0:T(8,128)S(1)} %collective-permute-done.10.refs_2_) | copy-start | bytes 393220
  157.2 9.7 %collective-permute-start.15 = (f32[64,512]{1,0:T(8,128)S(1)}, f32[64,512]{1,0:T(8,128)S(1)}, u32[]{:S(2)}, u32[]{:S(2)}) collective-permute-start(f32[64,512]{1,0:T(8,128)S(1)} %get-tuple-element.26), channel_id=1, source_target_pairs={{0,7},{1,6},{2,1},{3,0},{4,3},{5,2},{6,5},{7,4},{8,15},{9,14},{10,... | collective-permute-start | bytes 393224 | tf_op jit(solution)/shard_map/ppermute | solution.py:55
  169.5 7.6 %collective-permute-start.22 = (bf16[64,512]{1,0:T(8,128)(2,1)}, bf16[64,512]{1,0:T(8,128)(2,1)S(1)}, u32[]{:S(2)}, u32[]{:S(2)}) collective-permute-start(bf16[64,512]{1,0:T(8,128)(2,1)} %total_rows.1.refs_0_), channel_id=1, source_target_pairs={{0,7},{1,6},{2,1},{3,0},{4,3},{5,2},{6,5},{7,4},{8,15},{9,14},{10,... | collective-permute-start | bytes 196616 | tf_op jit(solution)/shard_map/ppermute | solution.py:55
  172.2 5.2 %collective-permute-start.21 = (bf16[64,512]{1,0:T(8,128)(2,1)}, bf16[64,512]{1,0:T(8,128)(2,1)S(1)}, u32[]{:S(2)}, u32[]{:S(2)}) collective-permute-start(bf16[64,512]{1,0:T(8,128)(2,1)} %total_rows.1.refs_0_), channel_id=1, source_target_pairs={{0,6},{1,7},{2,0},{3,1},{4,2},{5,3},{6,4},{7,5},{8,14},{9,15},{10,... | collective-permute-start | bytes 196616 | tf_op jit(solution)/shard_map/ppermute | solution.py:55
  173.4 5.7 %collective-permute-start.20 = (bf16[64,512]{1,0:T(8,128)(2,1)}, bf16[64,512]{1,0:T(8,128)(2,1)S(1)}, u32[]{:S(2)}, u32[]{:S(2)}) collective-permute-start(bf16[64,512]{1,0:T(8,128)(2,1)} %total_rows.1.refs_0_), channel_id=1, source_target_pairs={{0,5},{1,4},{2,7},{3,6},{4,1},{5,0},{6,3},{7,2},{8,13},{9,12},{10,... | collective-permute-start | bytes 196616 | tf_op jit(solution)/shard_map/ppermute | solution.py:55
  174.1 6.4 %collective-permute-start.19 = (bf16[64,512]{1,0:T(8,128)(2,1)}, bf16[64,512]{1,0:T(8,128)(2,1)S(1)}, u32[]{:S(2)}, u32[]{:S(2)}) collective-permute-start(bf16[64,512]{1,0:T(8,128)(2,1)} %total_rows.1.refs_0_), channel_id=1, source_target_pairs={{0,4},{1,5},{2,6},{3,7},{4,0},{5,1},{6,2},{7,3},{8,12},{9,13},{10,... | collective-permute-start | bytes 196616 | tf_op jit(solution)/shard_map/ppermute | solution.py:55
  175.9 5.3 %collective-permute-start.18 = (bf16[64,512]{1,0:T(8,128)(2,1)}, bf16[64,512]{1,0:T(8,128)(2,1)S(1)}, u32[]{:S(2)}, u32[]{:S(2)}) collective-permute-start(bf16[64,512]{1,0:T(8,128)(2,1)} %total_rows.1.refs_0_), channel_id=1, source_target_pairs={{0,3},{1,2},{2,5},{3,4},{4,7},{5,6},{6,1},{7,0},{8,11},{9,10},{10,... | collective-permute-start | bytes 196616 | tf_op jit(solution)/shard_map/ppermute | solution.py:55
  177.2 6.3 %collective-permute-start.17 = (bf16[64,512]{1,0:T(8,128)(2,1)}, bf16[64,512]{1,0:T(8,128)(2,1)S(1)}, u32[]{:S(2)}, u32[]{:S(2)}) collective-permute-start(bf16[64,512]{1,0:T(8,128)(2,1)} %total_rows.1.refs_0_), channel_id=1, source_target_pairs={{0,2},{1,3},{2,4},{3,5},{4,6},{5,7},{6,0},{7,1},{8,10},{9,11},{10,... | collective-permute-start | bytes 196616 | tf_op jit(solution)/shard_map/ppermute | solution.py:55
  177.4 6.1 %collective-permute-start.16 = (bf16[64,512]{1,0:T(8,128)(2,1)}, bf16[64,512]{1,0:T(8,128)(2,1)S(1)}, u32[]{:S(2)}, u32[]{:S(2)}) collective-permute-start(bf16[64,512]{1,0:T(8,128)(2,1)} %total_rows.1.refs_0_), channel_id=1, source_target_pairs={{0,1},{1,0},{2,3},{3,2},{4,5},{5,4},{6,7},{7,6},{8,9},{9,8},{10,11... | collective-permute-start | bytes 196616 | tf_op jit(solution)/shard_map/ppermute | solution.py:55
  (24 other events, 71.3 us)
